TPU v7x, 32 devices: a whole 2x2x4 slice. The times are simulated.
32 devices in a mesh: ctx: 4 (over x, core), fsdp: 8 (over z, y).
Axes of the slice: x: 2, y: 2, z: 4, core: 2. Of those that a mesh axis runs over, the one named last changes fastest.
Arguments:
- hidden_in: bfloat16 [2, 2, 4, 512, 2048], P(None, None, 'ctx', 'fsdp'), may hold values from -6 to 6
- cotangent: bfloat16 [2, 2, 4, 512, 2048], P(None, None, 'ctx', 'fsdp'), may hold values from -6 to 6
- routes: int32 [2, 2, 4, 512, 4], P(None, None, 'ctx', 'fsdp'), may hold values from 0 to 7, all different within a row
- priority: int32 [2, 2, 4, 512], P(None, None, 'ctx', 'fsdp'), may hold values from 0 to 1048575
- gain_attn: bfloat16 [2048], P('fsdp'), may hold values from 0.5 to 1.5
- attention_input_weights: bfloat16 [3, 2048, 2048], P(None, None, 'fsdp'), may hold values from -0.125 to 0.125
- attention_output_weights: bfloat16 [2048, 2048], P('fsdp'), may hold values from -0.5 to 0.5
- gain_ffn: bfloat16 [2048], P('fsdp'), may hold values from 0.5 to 1.5
- router: bfloat16 [2048, 8], P('fsdp'), may hold values from -0.0625 to 0.0625
- shared_gate: bfloat16 [2048], P('fsdp'), may hold values from -0.125 to 0.125
- shared_in: bfloat16 [2, 5632, 2048], P(None, 'fsdp'), may hold values from -0.125 to 0.125
- shared_out: bfloat16 [5632, 2048], P('fsdp'), may hold values from -0.15625 to 0.15625
- expert_in: bfloat16 [8, 2, 1408, 2048], P(None, None, 'fsdp'), may hold values from -0.125 to 0.125
- expert_out: bfloat16 [8, 1408, 2048], P(None, 'fsdp'), may hold values from -0.3125 to 0.3125
Outputs:
- layer_out: bfloat16 [2, 2, 4, 512, 2048], P(None, None, 'ctx', 'fsdp')
- grad_hidden: bfloat16 [2, 2, 4, 512, 2048], P(None, None, 'ctx', 'fsdp')
- grad_gain_attn: float32 [2048], P('fsdp')
- grad_attn_in: float32 [3, 2048, 2048], P(None, None, 'fsdp')
- grad_attn_out: float32 [2048, 2048], P('fsdp')
- grad_gain_ffn: float32 [2048], P('fsdp')
- grad_router: float32 [2048, 8], P('fsdp')
- grad_shared_gate: float32 [2048], P('fsdp')
- grad_shared_in: float32 [2, 5632, 2048], P(None, 'fsdp')
- grad_shared_out: float32 [5632, 2048], P('fsdp')
- grad_expert_in: float32 [8, 2, 1408, 2048], P(None, None, 'fsdp')
- grad_expert_out: float32 [8, 1408, 2048], P(None, 'fsdp')
Inputs may be any that keep to these rules, and one draw needn't show every extreme that they name: `routes`: each token names 4 different experts.
All inputs are finite; a program needn't handle non-finite values.
Results may differ from a plain program's by a relative error of at most 0.025.
Values may be sent and summed in bfloat16 or wider, within the bound.
A program may use at most 640 MiB of HBM per device.

v0:
```python
import jax
import jax.numpy as jnp
from jax import lax
from jax.sharding import PartitionSpec as P

HEAD_DIM = 128
BLOCK = 256


EPSILON = 1e-06
ROPE_BASE = 1000000.0
MASKED = -1e30
EXACT_PRECISION = lax.Precision.HIGHEST


def rope_tables(positions, head_size):
    halves = jnp.arange(head_size // 2, dtype=jnp.float32)
    frequency = ROPE_BASE ** (-2.0 * halves / head_size)
    angles = positions.astype(jnp.float32)[:, None] * frequency[None, :]
    return (jnp.cos(angles), jnp.sin(angles))


def rotate(values, cosine, sine, direction):
    middle = values.shape[-1] // 2
    first_half = values[..., :middle]
    second_half = values[..., middle:]
    cos_rows = cosine[:, None, :]
    sin_rows = sine[:, None, :] * direction
    return jnp.concatenate(
        [
            first_half * cos_rows - second_half * sin_rows,
            second_half * cos_rows + first_half * sin_rows,
        ],
        axis=-1,
    )


def softmax_rows(logits):
    highest = jnp.max(logits, axis=-1, keepdims=True)
    raised = jnp.exp(logits - highest)
    return raised / jnp.sum(raised, axis=-1, keepdims=True)


def dispatch_table(route_rows, order_keys, experts, capacity):
    count = order_keys.shape[0]
    row_index = jnp.arange(count, dtype=jnp.int32)
    before = (order_keys[None, :] < order_keys[:, None]) | (
        order_keys[None, :] == order_keys[:, None]
    ) & (row_index[None, :] < row_index[:, None])
    chosen = route_rows[:, :, None] == jnp.arange(experts, dtype=jnp.int32)[None, None, :]
    naming = jnp.sum(chosen.astype(jnp.int32), axis=1, dtype=jnp.int32)
    ahead = jnp.dot(
        before.astype(jnp.bfloat16), naming.astype(jnp.bfloat16), preferred_element_type=jnp.float32
    ).astype(jnp.int32)
    slots = jnp.sum(jnp.where(chosen, ahead[:, None, :], 0), axis=2, dtype=jnp.int32)
    placed = slots[:, :, None] == jnp.arange(capacity, dtype=jnp.int32)[None, None, :]
    return jnp.einsum("rke,rkc->ecr", chosen.astype(jnp.float32), placed.astype(jnp.float32))


def attend(query_rows, key_rows, value_rows, allowed, score_scale):
    scores = (
        jnp.einsum("qhd,khd->hqk", query_rows, key_rows, preferred_element_type=jnp.float32)
        * score_scale
    )
    scores = jnp.where(allowed[None], scores, MASKED)
    highest = jnp.max(scores, axis=-1, keepdims=True)
    raised = jnp.exp(scores - highest)
    totals = jnp.sum(raised, axis=-1, keepdims=True)
    weights = raised / totals
    mixed_result = jnp.einsum(
        "hqk,khd->qhd", weights.astype(jnp.bfloat16), value_rows, preferred_element_type=jnp.float32
    )
    return (mixed_result.astype(jnp.bfloat16), highest + jnp.log(totals))


def attend_back(query_rows, key_rows, value_rows, log_totals, grad_mixed, allowed, score_scale):
    scores = (
        jnp.einsum("qhd,khd->hqk", query_rows, key_rows, preferred_element_type=jnp.float32)
        * score_scale
    )
    scores = jnp.where(allowed[None], scores, MASKED)
    weights = jnp.exp(scores - log_totals)
    grad_weights = jnp.einsum(
        "qhd,khd->hqk", grad_mixed, value_rows, preferred_element_type=jnp.float32
    )
    grad_values = jnp.einsum(
        "hqk,qhd->khd", weights.astype(jnp.bfloat16), grad_mixed, preferred_element_type=jnp.float32
    )
    grad_scores = (
        weights * (grad_weights - jnp.sum(weights * grad_weights, axis=-1, keepdims=True))
    ).astype(jnp.bfloat16)
    grad_query = (
        jnp.einsum("hqk,khd->qhd", grad_scores, key_rows, preferred_element_type=jnp.float32)
        * score_scale
    )
    grad_keys = (
        jnp.einsum("hqk,qhd->khd", grad_scores, query_rows, preferred_element_type=jnp.float32)
        * score_scale
    )
    return (grad_query, grad_keys, grad_values)


def ffn_forward(rows_in, inner, outer):
    gate_val = jnp.einsum(
        "...nd,...fd->...nf", rows_in, inner[..., 0, :, :], preferred_element_type=jnp.float32
    )
    up_val = jnp.einsum(
        "...nd,...fd->...nf", rows_in, inner[..., 1, :, :], preferred_element_type=jnp.float32
    )
    activated = (jax.nn.silu(gate_val) * up_val).astype(jnp.bfloat16)
    result = jnp.einsum("...nf,...fd->...nd", activated, outer, preferred_element_type=jnp.float32)
    return (result, gate_val, up_val, activated)


def ffn_backward(grad_rows, rows_in, inner, outer, gate_val, up_val, activated):
    grad_act = jnp.einsum(
        "...nd,...fd->...nf", grad_rows, outer, preferred_element_type=jnp.float32
    )
    sigmoid_val = jax.nn.sigmoid(gate_val)
    grad_gate = (grad_act * up_val * sigmoid_val * (1.0 + gate_val * (1.0 - sigmoid_val))).astype(
        jnp.bfloat16
    )
    grad_up = (grad_act * gate_val * sigmoid_val).astype(jnp.bfloat16)
    grad_inner = jnp.stack(
        [
            jnp.einsum(
                "...nf,...nd->...fd", grad_gate, rows_in, preferred_element_type=jnp.float32
            ),
            jnp.einsum("...nf,...nd->...fd", grad_up, rows_in, preferred_element_type=jnp.float32),
        ],
        axis=-3,
    )
    grad_outer = jnp.einsum(
        "...nf,...nd->...fd", activated, grad_rows, preferred_element_type=jnp.float32
    )
    grad_input = jnp.einsum(
        "...nf,...fd->...nd", grad_gate, inner[..., 0, :, :], preferred_element_type=jnp.float32
    )
    grad_input = grad_input + jnp.einsum(
        "...nf,...fd->...nd", grad_up, inner[..., 1, :, :], preferred_element_type=jnp.float32
    )
    return (grad_input, grad_inner, grad_outer)


def norm_back(grad_normed, values, inverse, gain_full):
    scaled = grad_normed * gain_full
    grad_values = inverse * (
        scaled - values * inverse * inverse * jnp.mean(scaled * values, axis=-1, keepdims=True)
    )
    grad_gain = jnp.sum(grad_normed * values * inverse, axis=0)
    return (grad_values, grad_gain)


def share_rows(token_rows, slot_rows):
    return (
        lax.all_gather(token_rows, "fsdp", axis=0, tiled=True),
        lax.all_gather(slot_rows, "fsdp", axis=1, tiled=True),
    )


def reduce_rows(token_part, slot_part):
    return (
        lax.psum_scatter(
            token_part.astype(jnp.bfloat16), "fsdp", scatter_dimension=0, tiled=True
        ).astype(jnp.float32),
        lax.psum_scatter(
            slot_part.astype(jnp.bfloat16), "fsdp", scatter_dimension=1, tiled=True
        ).astype(jnp.float32),
    )


def per_device(
    hidden_in,
    cotangent,
    routes,
    priority,
    gain_attn,
    attention_input_weights,
    attention_output_weights,
    gain_ffn,
    router,
    shared_gate,
    shared_in,
    shared_out,
    expert_in,
    expert_out,
):
    shard_count = lax.axis_size("fsdp")
    ctx_count = lax.axis_size("ctx")
    ctx_index = lax.axis_index("ctx")
    seq_count = hidden_in.shape[0]
    part_rows = hidden_in.shape[3]
    width = hidden_in.shape[4]
    block_rows = part_rows * shard_count
    pair_rows = 2 * block_rows
    group_rows = seq_count * pair_rows
    own_rows = seq_count * 2 * part_rows
    local_width = attention_input_weights.shape[2]
    heads_local = local_width // HEAD_DIM
    seq_length = 2 * ctx_count * block_rows
    expert_count = expert_in.shape[0]
    top_count = routes.shape[-1]
    capacity = 5 * own_rows * top_count // (4 * expert_count)
    score_scale = HEAD_DIM ** (-0.5)
    gathered_in, gain_one = (
        lax.all_gather(hidden_in, "fsdp", axis=3, tiled=True),
        lax.all_gather(gain_attn, "fsdp", axis=0, tiled=True),
    )
    group_in = gathered_in.reshape(group_rows, width).astype(jnp.float32)
    inverse_group = lax.rsqrt(jnp.mean(group_in * group_in, axis=-1, keepdims=True) + EPSILON)
    gain_one_f = gain_one.astype(jnp.float32)
    normed_one = (group_in * inverse_group * gain_one_f).astype(jnp.bfloat16)
    projected_rows = jnp.einsum(
        "nd,jde->jne", normed_one, attention_input_weights, preferred_element_type=jnp.float32
    )
    pair_index = jnp.arange(pair_rows, dtype=jnp.int32)
    query_unit = jnp.where(pair_index < block_rows, ctx_index, 2 * ctx_count - 1 - ctx_index)
    positions = query_unit * block_rows + pair_index % block_rows
    cosine, sine = rope_tables(positions, HEAD_DIM)
    key_block = jnp.arange(seq_length, dtype=jnp.int32) // BLOCK
    allowed = key_block[None, :] <= (positions // BLOCK)[:, None]
    shaped = projected_rows.reshape(3, seq_count, pair_rows, heads_local, HEAD_DIM)
    query = rotate(shaped[0], cosine, sine, 1.0).astype(jnp.bfloat16)
    key_rows = rotate(shaped[1], cosine, sine, 1.0).astype(jnp.bfloat16)
    value_rows = shaped[2].astype(jnp.bfloat16)
    key_pair = jnp.stack([key_rows, value_rows]).reshape(
        2, seq_count, 2, 1, block_rows, local_width
    )
    all_pairs = lax.all_gather(key_pair, "ctx", axis=3, tiled=True)
    ordered = jnp.concatenate([all_pairs[:, :, 0], jnp.flip(all_pairs[:, :, 1], axis=2)], axis=2)
    ordered = ordered.reshape(2, seq_count, seq_length, heads_local, HEAD_DIM)

    def forward_seq(carry, seq_items):
        mixed_one, total_one = attend(
            seq_items[0], seq_items[1], seq_items[2], allowed, score_scale
        )
        return (carry, (mixed_one, total_one))

    _, (mixed_all, log_totals) = lax.scan(forward_seq, 0, (query, ordered[0], ordered[1]))
    mixed_rows = mixed_all.reshape(group_rows, local_width)
    attention_contribution = jnp.dot(
        mixed_rows, attention_output_weights, preferred_element_type=jnp.float32
    ).reshape(seq_count, 2, 1, block_rows, width)
    attn_own = lax.psum_scatter(attention_contribution, "fsdp", scatter_dimension=3, tiled=True)
    resid_in = hidden_in.reshape(own_rows, width).astype(jnp.float32)
    resid_mid = resid_in + attn_own.reshape(own_rows, width)
    gain_two, router_full, shared_vector = (
        lax.all_gather(gain_ffn, "fsdp", axis=0, tiled=True),
        lax.all_gather(router, "fsdp", axis=0, tiled=True),
        lax.all_gather(shared_gate, "fsdp", axis=0, tiled=True),
    )
    gain_two_f = gain_two.astype(jnp.float32)
    inverse_two = lax.rsqrt(jnp.mean(resid_mid * resid_mid, axis=-1, keepdims=True) + EPSILON)
    normed_two = (resid_mid * inverse_two * gain_two_f).astype(jnp.bfloat16)
    logits = jnp.dot(normed_two, router_full, preferred_element_type=jnp.float32)
    gates = softmax_rows(logits)
    shared_weight = jax.nn.sigmoid(
        jnp.dot(normed_two, shared_vector, preferred_element_type=jnp.float32)
    )
    table = dispatch_table(
        routes.reshape(own_rows, top_count), priority.reshape(own_rows), expert_count, capacity
    )
    buffers = jnp.einsum(
        "ecr,rd->ecd", table.astype(jnp.bfloat16), normed_two, preferred_element_type=jnp.float32
    ).astype(jnp.bfloat16)
    all_tokens, all_buffers = share_rows(normed_two, buffers)
    shared_piece, shared_gate_val, shared_up_val, shared_act = ffn_forward(
        all_tokens, shared_in, shared_out
    )
    expert_piece, expert_gate_val, expert_up_val, expert_act = ffn_forward(
        all_buffers, expert_in, expert_out
    )
    shared_part, expert_res = reduce_rows(shared_piece, expert_piece)
    flat_res = expert_res.reshape(expert_count * capacity, width)
    mixing = (gates.T[:, None, :] * table).reshape(expert_count * capacity, own_rows)
    moe = jnp.einsum("xr,xd->rd", mixing, flat_res, precision=EXACT_PRECISION)
    result_rows = resid_mid + moe + shared_weight[:, None] * shared_part
    layer_out = result_rows.astype(jnp.bfloat16).reshape(hidden_in.shape)
    grad_out = cotangent.reshape(own_rows, width).astype(jnp.float32)
    grad_shared = (grad_out * shared_weight[:, None]).astype(jnp.bfloat16)
    grad_logit_s = jnp.sum(grad_out * shared_part, axis=-1) * shared_weight * (1.0 - shared_weight)
    grad_shared_vector = jnp.einsum(
        "r,rd->d", grad_logit_s, normed_two.astype(jnp.float32), precision=EXACT_PRECISION
    )
    grad_normed = grad_logit_s[:, None] * shared_vector.astype(jnp.float32)[None, :]
    grad_mixing = jnp.einsum("rd,xd->xr", grad_out, flat_res, precision=EXACT_PRECISION)
    grad_gates = jnp.sum(grad_mixing.reshape(expert_count, capacity, own_rows) * table, axis=1).T
    grad_res = (
        jnp.einsum("xr,rd->xd", mixing, grad_out, precision=EXACT_PRECISION)
        .reshape(expert_count, capacity, width)
        .astype(jnp.bfloat16)
    )
    grad_logits = (
        gates * (grad_gates - jnp.sum(gates * grad_gates, axis=-1, keepdims=True))
    ).astype(jnp.bfloat16)
    grad_router = jnp.einsum(
        "rd,re->de", normed_two, grad_logits, preferred_element_type=jnp.float32
    )
    grad_normed = grad_normed + jnp.einsum(
        "re,de->rd", grad_logits, router_full, preferred_element_type=jnp.float32
    )
    all_grad_shared, all_grad_res = share_rows(grad_shared, grad_res)
    shared_back, grad_shared_in, grad_shared_out = ffn_backward(
        all_grad_shared,
        all_tokens,
        shared_in,
        shared_out,
        shared_gate_val,
        shared_up_val,
        shared_act,
    )
    expert_back, grad_expert_in, grad_expert_out = ffn_backward(
        all_grad_res, all_buffers, expert_in, expert_out, expert_gate_val, expert_up_val, expert_act
    )
    grad_rows_shared, grad_buffers = reduce_rows(shared_back, expert_back)
    grad_normed = (
        grad_normed
        + grad_rows_shared
        + jnp.einsum("ecr,ecd->rd", table, grad_buffers, precision=EXACT_PRECISION)
    )
    grad_mid_norm, grad_gain_two = norm_back(grad_normed, resid_mid, inverse_two, gain_two_f)
    grad_mid = grad_out + grad_mid_norm
    grad_branch = grad_mid.astype(jnp.bfloat16).reshape(seq_count, 2, 1, part_rows, width)
    all_grad_branch = lax.all_gather(grad_branch, "fsdp", axis=3, tiled=True).reshape(
        group_rows, width
    )
    grad_attn_out = jnp.einsum(
        "nk,nd->kd", mixed_rows, all_grad_branch, preferred_element_type=jnp.float32
    )
    grad_mixed = jnp.einsum(
        "nd,kd->nk", all_grad_branch, attention_output_weights, preferred_element_type=jnp.float32
    )
    grad_mixed = grad_mixed.astype(jnp.bfloat16).reshape(
        seq_count, pair_rows, heads_local, HEAD_DIM
    )

    def backward_seq(carry, seq_items):
        return (
            carry,
            attend_back(
                seq_items[0],
                seq_items[1],
                seq_items[2],
                seq_items[3],
                seq_items[4],
                allowed,
                score_scale,
            ),
        )

    _, (grad_query, grad_keys, grad_values) = lax.scan(
        backward_seq, 0, (query, ordered[0], ordered[1], log_totals, grad_mixed)
    )
    pair_grads = jnp.stack([grad_keys, grad_values]).reshape(
        2, seq_count, 2 * ctx_count, block_rows, local_width
    )
    dealt_grads = jnp.stack(
        [pair_grads[:, :, :ctx_count], jnp.flip(pair_grads[:, :, ctx_count:], axis=2)], axis=2
    )
    owned_pairs = (
        lax.psum_scatter(dealt_grads.astype(jnp.bfloat16), "ctx", scatter_dimension=3, tiled=True)
        .astype(jnp.float32)
        .reshape(2, seq_count, pair_rows, heads_local, HEAD_DIM)
    )
    grad_q_raw = rotate(grad_query, cosine, sine, -1.0).astype(jnp.bfloat16)
    grad_k_raw = rotate(owned_pairs[0], cosine, sine, -1.0).astype(jnp.bfloat16)
    grad_v_raw = owned_pairs[1].astype(jnp.bfloat16)
    raw_grads = jnp.stack([grad_q_raw, grad_k_raw, grad_v_raw]).reshape(3, group_rows, local_width)
    grad_attn_in = jnp.einsum(
        "nd,jne->jde", normed_one, raw_grads, preferred_element_type=jnp.float32
    )
    grad_normed_one = jnp.einsum(
        "jne,jde->nd", raw_grads, attention_input_weights, preferred_element_type=jnp.float32
    )
    grad_normed_one = lax.psum_scatter(
        grad_normed_one.reshape(seq_count, 2, 1, block_rows, width).astype(jnp.bfloat16),
        "fsdp",
        scatter_dimension=3,
        tiled=True,
    ).astype(jnp.float32)
    inverse_own = lax.rsqrt(jnp.mean(resid_in * resid_in, axis=-1, keepdims=True) + EPSILON)
    grad_in_norm, grad_gain_one = norm_back(
        grad_normed_one.reshape(own_rows, width), resid_in, inverse_own, gain_one_f
    )
    grad_hidden = (grad_mid + grad_in_norm).astype(jnp.bfloat16).reshape(hidden_in.shape)
    small_parts = (
        lax.psum_scatter(
            grad_gain_one.astype(jnp.bfloat16), "fsdp", scatter_dimension=0, tiled=True
        ).astype(jnp.float32),
        lax.psum_scatter(
            grad_gain_two.astype(jnp.bfloat16), "fsdp", scatter_dimension=0, tiled=True
        ).astype(jnp.float32),
        lax.psum_scatter(
            grad_router.astype(jnp.bfloat16), "fsdp", scatter_dimension=0, tiled=True
        ).astype(jnp.float32),
        lax.psum_scatter(
            grad_shared_vector.astype(jnp.bfloat16), "fsdp", scatter_dimension=0, tiled=True
        ).astype(jnp.float32),
    )
    totals = (
        lax.psum(small_parts[0].astype(jnp.bfloat16), "ctx").astype(jnp.float32),
        lax.psum(small_parts[1].astype(jnp.bfloat16), "ctx").astype(jnp.float32),
        lax.psum(small_parts[2].astype(jnp.bfloat16), "ctx").astype(jnp.float32),
        lax.psum(small_parts[3].astype(jnp.bfloat16), "ctx").astype(jnp.float32),
        lax.psum(grad_attn_in.astype(jnp.bfloat16), "ctx").astype(jnp.float32),
        lax.psum(grad_attn_out.astype(jnp.bfloat16), "ctx").astype(jnp.float32),
        lax.psum(grad_shared_in.astype(jnp.bfloat16), "ctx").astype(jnp.float32),
        lax.psum(grad_shared_out.astype(jnp.bfloat16), "ctx").astype(jnp.float32),
        lax.psum(grad_expert_in.astype(jnp.bfloat16), "ctx").astype(jnp.float32),
        lax.psum(grad_expert_out.astype(jnp.bfloat16), "ctx").astype(jnp.float32),
    )
    return (
        layer_out,
        grad_hidden,
        totals[0],
        totals[4],
        totals[5],
        totals[1],
        totals[2],
        totals[3],
        totals[6],
        totals[7],
        totals[8],
        totals[9],
    )


def solution(mesh):
    placed = (
        P(None, None, "ctx", "fsdp", None),
        P(None, None, "ctx", "fsdp", None),
        P(None, None, "ctx", "fsdp", None),
        P(None, None, "ctx", "fsdp"),
        P("fsdp"),
        P(None, None, "fsdp"),
        P("fsdp", None),
        P("fsdp"),
        P("fsdp", None),
        P("fsdp"),
        P(None, "fsdp", None),
        P("fsdp", None),
        P(None, None, "fsdp", None),
        P(None, "fsdp", None),
    )
    return jax.shard_map(
        per_device,
        mesh=mesh,
        in_specs=placed,
        out_specs=(
            P(None, None, "ctx", "fsdp", None),
            P(None, None, "ctx", "fsdp", None),
            P("fsdp"),
            P(None, None, "fsdp"),
            P("fsdp", None),
            P("fsdp"),
            P("fsdp", None),
            P("fsdp"),
            P(None, "fsdp", None),
            P("fsdp", None),
            P(None, None, "fsdp", None),
            P(None, "fsdp", None),
        ),
        check_vma=False,
    )
```

profile of v0, /device:TPU:0, one launch (start us, length us, event | category | flops | bytes accessed | tf_op | source)
XLA Modules:
  0.0 5600.4 jit_solution(11005720815096267817)
XLA Ops:
  34.4 103.6 %all-gather.11.cloned.1.call-done = bf16[2,2,1,512,2048]{4,3,2,1,0:T(8,128)(2,1)} async-done(((bf16[2,2,1,64,2048]{4,3,2,1,0:T(8,128)(2,1)}), bf16[2,2,1,512,2048]{4,3,2,1,0:T(8,128)(2,1)}) %all-gather.11.cloned.1.call-update) | async-done | bytes 8388624 | tf_op jit(solution)/shard_map/all_gather | solution.py:206
  193.9 51.4 all-gather.13.cloned.1.call-done
  298.4 109.1 %while.28 = (s32[]{:T(128)}, bf16[2,1024,2,128]{1,3,2,0:T(8,128)(2,1)}, f32[2,2,1024,1]{2,1,3,0:T(2,128)S(1)}, bf16[2,4096,2,128]{1,3,2,0:T(8,128)(2,1)}, bf16[2...) while((s32[]{:T(128)}, ...), condition=%wide.region_4.5_spmd.clone, body=%wide.region_1.4_spmd.clone.sunk | while | flops 4400084992 | bytes 164714704 | solution.py:239
  450.6 263.6 %reduce-scatter.11.cloned.1.call-done = f32[2,2,1,64,2048]{4,3,1,0,2:T(8,128)} async-done(((f32[2,2,1,512,2048]{4,3,1,0,2:T(8,128)}), f32[2,2,1,64,2048]{4,3,1,0,2:T(8,128)}) %reduce-scatter.11.cloned.1.call-update) | async-done | bytes 2097168 | tf_op jit(solution)/shard_map/reduce_scatter | solution.py:244
  721.2 124.0 %all-gather.17.cloned.1.call-done = bf16[2048,2048]{1,0:T(8,128)(2,1)} async-done(((bf16[256,2048]{1,0:T(8,128)(2,1)}), bf16[2048,2048]{1,0:T(8,128)(2,1)}) %all-gather.17.cloned.1.call-update) | async-done | bytes 8388624 | tf_op jit(solution)/shard_map/all_gather | solution.py:156
  895.6 31.9 all_gather.37
  960.7 63.4 %reduce-scatter.15.cloned.1.call-done = bf16[256,2048]{1,0:T(8,128)(2,1)} async-done(((bf16[2048,2048]{1,0:T(8,128)(2,1)}), bf16[256,2048]{1,0:T(8,128)(2,1)}) %reduce-scatter.15.cloned.1.call-update) | async-done | bytes 1048592 | tf_op jit(solution)/shard_map/reduce_scatter | solution.py:163
  1029.7 790.5 %all-gather.15.cloned.1.call-done = bf16[8,1280,2048]{2,1,0:T(8,128)(2,1)} async-done(((bf16[8,160,2048]{2,1,0:T(8,128)(2,1)}), bf16[8,1280,2048]{2,1,0:T(8,128)(2,1)}) %all-gather.15.cloned.1.call-update) | async-done | bytes 41943056 | tf_op jit(solution)/shard_map/all_gather | solution.py:157
  1867.2 749.6 %all-gather.21.cloned.1.call-done = bf16[8,1280,2048]{2,1,0:T(8,128)(2,1)} async-done(((bf16[8,160,2048]{2,1,0:T(8,128)(2,1)}), bf16[8,1280,2048]{2,1,0:T(8,128)(2,1)}) %all-gather.21.cloned.1.call-update) | async-done | bytes 41943056 | tf_op jit(solution)/shard_map/all_gather | solution.py:157
  2616.7 29.6 multiply_convert_fusion.1
  2666.6 32.8 fusion.76
  2699.4 43.9 add_convert_fusion
  2786.3 626.9 %reduce-scatter.13.cloned.1.call-done = bf16[8,160,2048]{2,1,0:T(8,128)(2,1)} async-done(((bf16[8,1280,2048]{2,1,0:T(8,128)(2,1)}), bf16[8,160,2048]{2,1,0:T(8,128)(2,1)}) %reduce-scatter.13.cloned.1.call-update) | async-done | bytes 5242896 | tf_op jit(solution)/shard_map/reduce_scatter | solution.py:166
  3418.1 664.5 %reduce-scatter.19.cloned.1.call-done = bf16[8,160,2048]{2,1,0:T(8,128)(2,1)} async-done(((bf16[8,1280,2048]{2,1,0:T(8,128)(2,1)}), bf16[8,160,2048]{2,1,0:T(8,128)(2,1)}) %reduce-scatter.19.cloned.1.call-update) | async-done | bytes 5242896 | tf_op jit(solution)/shard_map/reduce_scatter | solution.py:166
  4091.1 143.9 %reduce-scatter.17.cloned.1.call-done = bf16[256,2048]{1,0:T(8,128)(2,1)} async-done(((bf16[2048,2048]{1,0:T(8,128)(2,1)}), bf16[256,2048]{1,0:T(8,128)(2,1)}) %reduce-scatter.17.cloned.1.call-update) | async-done | bytes 1048592 | tf_op jit(solution)/shard_map/reduce_scatter | solution.py:163
  4316.8 48.4 all-gather.23.cloned.1.call-done
  4374.4 241.3 %while.29 = (s32[]{:T(128)}, f32[2,1024,2,128]{3,2,1,0:T(2,128)}, bf16[2,4096,2,128]{1,3,2,0:T(8,128)(2,1)}, bf16[2,4096,2,128]{1,3,2,0:T(8,128)(2,1)}, bf16[2,4...) while((s32[]{:T(128)}, f32[2,1024,2,128]{3,2,1,0:T(2,128)}, ...), condition=%wide.region_22.23_spmd.clone, body=%wide.region_20.22_spmd.clone.sunk | while | flops 10868750336 | bytes 329332928 | solution.py:351
  4412.8 26.7 multiply_reduce_fusion.5
  4439.5 28.1 multiply_convert_fusion.9
  4559.8 28.1 multiply_convert_fusion.9
  4696.9 113.0 %all-reduce.10.cloned.1.call-done = bf16[2,2,2,4,512,256]{5,4,3,1,0,2:T(8,128)(2,1)} async-done(((bf16[2,2,2,4,512,256]{5,4,3,1,0,2:T(8,128)(2,1)}), bf16[2,2,2,4,512,256]{5,4,3,1,0,2:T(8,128)(2,1)}) %all-reduce.10.cloned.1.call-update) | async-done | bytes 8388624
  4906.3 463.9 %all-reduce.12.cloned.1.call-done = (bf16[3,2048,256]{1,2,0:T(8,128)(2,1)}, bf16[8,2,176,2048]{3,2,0,1:T(8,128)(2,1)}, bf16[256,2048]{1,0:T(8,128)(2,1)}, bf16[2...) async-done(((bf16[3,2048,256]{1,2,0:T(8,128)(2,1)}, bf16[8,2,176,2048]{3,2,0,1:T(8,128)(2,1)}, bf16[256,2048]{1,0:T(8,128)(2,1)}, ...) | async-done | bytes 30146576 | tf_op jit(solution)/shard_map/psum | solution.py:405
  5406.9 116.5 %reduce-scatter.21.cloned.1.call-done = bf16[2,2,1,64,2048]{4,3,1,0,2:T(8,128)(2,1)} async-done(((bf16[2,2,1,512,2048]{4,3,1,0,2:T(8,128)(2,1)}), bf16[2,2,1,64,2048]{4,3,1,0,2:T(8,128)(2,1)}) %reduce-scatter.21.cloned.1.call-update) | async-done | bytes 1048592 | tf_op jit(solution)/shard_map/reduce_scatter | solution.py:375
  5525.5 35.2 all-reduce.4
  (364 shorter events, 1004.3 us)
Async XLA Ops:
  7.2 130.8 %all-gather.11.cloned.1.call-start = ((), (), s32[]{:S(2)}) async-start(), calls=%async_computation.7 | async-start | bytes 9437184 | tf_op jit(solution)/shard_map/all_gather | solution.py:206
  7.9 237.3 %all-gather.13.cloned.1.call-start = ((), (), s32[]{:S(2)}) async-start(), calls=%async_computation.8 | async-start | bytes 10485760 | tf_op jit(solution)/shard_map/all_gather | solution.py:229
  188.6 525.6 %reduce-scatter.11.cloned.1.call-start = ((), (), s32[]{:S(2)}) async-start(), calls=%async_computation.9 | async-start | bytes 18874368 | tf_op jit(solution)/shard_map/reduce_scatter | solution.py:244
  429.3 415.9 %all-gather.17.cloned.1.call-start = ((), (), s32[]{:S(2)}) async-start(), calls=%async_computation.12 | async-start | bytes 9437184 | tf_op jit(solution)/shard_map/all_gather | solution.py:156
  721.1 303.0 %reduce-scatter.15.cloned.1.call-start = ((), (), s32[]{:S(2)}) async-start(), calls=%async_computation.13 | async-start | bytes 9437184 | tf_op jit(solution)/shard_map/reduce_scatter | solution.py:163
  876.4 943.7 %all-gather.15.cloned.1.call-start = ((), (), s32[]{:S(2)}) async-start(), calls=%async_computation.10 | async-start | bytes 47185920 | tf_op jit(solution)/shard_map/all_gather | solution.py:157
  895.0 1721.7 %all-gather.21.cloned.1.call-start = ((), (), s32[]{:S(2)}) async-start(), calls=%async_computation.16 | async-start | bytes 47185920 | tf_op jit(solution)/shard_map/all_gather | solution.py:157
  939.8 1804.6 %all-gather.19.cloned.1.call-start = ((), (), s32[]{:S(2)}) async-start(), calls=%async_computation.14 | async-start | bytes 9437184 | tf_op jit(solution)/shard_map/all_gather | solution.py:156
  1029.6 2383.6 %reduce-scatter.13.cloned.1.call-start = ((), (), s32[]{:S(2)}) async-start(), calls=%async_computation.11 | async-start | bytes 47185920 | tf_op jit(solution)/shard_map/reduce_scatter | solution.py:166
  2666.5 1416.1 %reduce-scatter.19.cloned.1.call-start = ((), (), s32[]{:S(2)}) async-start(), calls=%async_computation.17 | async-start | bytes 47185920 | tf_op jit(solution)/shard_map/reduce_scatter | solution.py:166
  2743.3 1491.7 %reduce-scatter.17.cloned.1.call-start = ((), (), s32[]{:S(2)}) async-start(), calls=%async_computation.15 | async-start | bytes 9437184 | tf_op jit(solution)/shard_map/reduce_scatter | solution.py:163
  2785.5 1579.6 %all-gather.23.cloned.1.call-start = ((), (), s32[]{:S(2)}) async-start(), calls=%async_computation.18 | async-start | bytes 9437184 | tf_op jit(solution)/shard_map/all_gather | solution.py:324
  2786.3 631.7 %copy-start.18 = (f32[256,8]{0,1:T(8,128)S(1)}, f32[256,8]{0,1:T(8,128)}, u32[]{:S(2)}) copy-start(f32[256,8]{0,1:T(8,128)} %copy-done.17) | copy-start | bytes 24580
  2786.3 631.7 %copy-start.33 = (f32[256]{0:T(256)S(1)}, f32[256]{0:T(256)}, u32[]{:S(2)}) copy-start(f32[256]{0:T(256)} %copy-done.32) | copy-start | bytes 3076
  2786.3 631.7 %copy-start.39 = (f32[256]{0:T(256)S(1)}, f32[256]{0:T(256)}, u32[]{:S(2)}) copy-start(f32[256]{0:T(256)} %copy-done.38) | copy-start | bytes 3076
  3418.0 817.0 %copy-start.28 = (bf16[256,8]{0,1:T(8,128)(2,1)}, bf16[256,8]{0,1:T(8,128)(2,1)S(1)}, u32[]{:S(2)}) copy-start(bf16[256,8]{0,1:T(8,128)(2,1)S(1)} %fusion.162) | copy-start | bytes 12292
  3418.0 817.0 %copy-start.16 = (bf16[2048,8]{0,1:T(8,128)(2,1)S(1)}, bf16[2048,8]{0,1:T(8,128)(2,1)}, u32[]{:S(2)}) copy-start(bf16[2048,8]{0,1:T(8,128)(2,1)} %copy-done.15) | copy-start | bytes 98308
  3418.0 817.0 %copy-start.20 = (f32[8,1,256]{2,1,0:T(1,128)S(1)}, f32[8,1,256]{2,1,0:T(1,128)}, u32[]{:S(2)}) copy-start(f32[8,1,256]{2,1,0:T(1,128)} %copy-done.19) | copy-start | bytes 24580
  3418.0 817.0 %copy-start.35 = (f32[256]{0:T(256)S(1)}, f32[256]{0:T(256)}, u32[]{:S(2)}) copy-start(f32[256]{0:T(256)} %copy-done.34) | copy-start | bytes 3076
  3418.1 817.0 %copy-start.42 = (f32[256]{0:T(256)S(1)}, f32[256]{0:T(256)}, u32[]{:S(2)}) copy-start(f32[256]{0:T(256)} %get-tuple-element.367) | copy-start | bytes 3076
  4241.1 568.8 %all-reduce.10.cloned.1.call-start = ((), (), s32[]{:S(2)}) async-start(), calls=%async_computation.21 | async-start | bytes 16777216
  4658.7 711.6 %all-reduce.12.cloned.1.call-start = ((), (), s32[]{:S(2)}) async-start(), calls=%async_computation.22 | async-start | bytes 60293120 | tf_op jit(solution)/shard_map/psum | solution.py:405
  4863.2 660.1 %reduce-scatter.21.cloned.1.call-start = ((), (), s32[]{:S(2)}) async-start(), calls=%async_computation.19 | async-start | bytes 9437184 | tf_op jit(solution)/shard_map/reduce_scatter | solution.py:375
  4891.2 688.6 %reduce-scatter.23.cloned.1.call-start = ((), (), s32[]{:S(2)}) async-start(), calls=%async_computation.20 | async-start | bytes 36864 | tf_op jit(solution)/shard_map/reduce_scatter | solution.py:393
  (68 other events, 1984.6 us)
Sparse Core Ops, SparseCore 0:
  10.2 127.7 all-gather.10
  188.7 56.4 all-gather.12
  429.4 284.7 reduce-scatter.10
  721.3 123.9 all-gather.16
  876.5 147.5 reduce-scatter.14
  1026.1 794.0 all-gather.14
  1821.7 794.9 all-gather.20
  2619.4 124.8 all-gather.18
  2748.2 664.9 reduce-scatter.12
  3417.4 665.1 reduce-scatter.18
  4086.8 148.1 reduce-scatter.16
  4241.2 123.9 all-gather.22
  4658.8 151.0 all-reduce.9
  4863.3 506.8 all-reduce.11
  5373.8 149.5 reduce-scatter.20
  5527.2 52.4 reduce-scatter.22
where the time goes:
time: 5610 us; the launch traced here: 5600 us
  waiting for transfers between devices  4340 us (77%)
  matrix products  664 us (12%)
  other arithmetic  255 us (5%)
  local copies, waits for them, and re-layouts  186 us (3%)
  blocking collectives  134 us (2%)
    all_gather x2, waiting for transfers between devices, share_rows(): lax.all_gather(slot_rows, 'fsdp', axis=1, tiled=True)  1540 us
    reduce_scatter x2, waiting for transfers between devices, reduce_rows(): lax.psum_scatter(slot_part.astype(jnp.bfloat16), 'fsdp', scatter_dimensio...  1290 us
    psum x1, waiting for transfers between devices, per_device(): lax.psum(grad_attn_in.astype(jnp.bfloat16), 'ctx').astype(jnp.float32)  464 us
    reduce_scatter x1, waiting for transfers between devices, per_device(): lax.psum_scatter(attention_contribution, 'fsdp', scatter_dimension=3, til...  264 us
    reduce_scatter x2, waiting for transfers between devices, reduce_rows(): lax.psum_scatter(token_part.astype(jnp.bfloat16), 'fsdp', scatter_dimensi...  207 us
    all_gather x2, waiting for transfers between devices, share_rows(): lax.all_gather(token_rows, 'fsdp', axis=0, tiled=True)  125 us
    reduce_scatter x1, waiting for transfers between devices, per_device(): lax.psum_scatter(grad_normed_one.reshape(seq_count, 2, 1, block_rows, wid...  116 us
    unnamed x17, waiting for transfers between devices  114 us
  transfers between devices with their start and end apart: 16, of which 16 were waited for; matrix products, arithmetic and copies ran while one was open for 8% of the time, Pallas kernels for 0%

commit v1 on v0

v1 whole, which is shorter than its diff:
```python
import functools

import jax
import jax.numpy as jnp
import numpy as np
from jax import lax
from jax.experimental import pallas as pl
from jax.experimental.pallas import tpu as pltpu
from jax.sharding import PartitionSpec as P

HEAD_DIM = 128
BLOCK = 256
EPSILON = 1e-06
ROPE_BASE = 1000000.0
LOG2E = 1.4426950408889634
EXACT = lax.Precision.HIGHEST
BF = jnp.bfloat16
F32 = jnp.float32
MIB = 1 << 20


def ring_order(count):
    if count == 8:
        return [0, 2, 4, 6, 7, 5, 3, 1]
    side = int(round(count**0.5))
    if side * side != count:
        return list(range(count))
    order = []
    for row in range(side):
        line = [row * side + col for col in range(side)]
        order += line if row % 2 == 0 else line[::-1]
    return order


def after(value, *others):
    return lax.optimization_barrier((value, *others))[0]


def dot(a, b, ca, cb):
    return lax.dot_general(a, b, (((ca,), (cb,)), ((), ())), preferred_element_type=F32)


def project_kernel(h_ref, gain_ref, w_ref, cos_ref, sin_ref, n_ref, q_ref, kv_ref):
    x = h_ref[...].astype(F32)
    inverse = lax.rsqrt(jnp.mean(x * x, axis=-1, keepdims=True) + EPSILON)
    normed = (x * inverse * gain_ref[...]).astype(BF)
    n_ref[...] = normed
    cosine, sine = cos_ref[...], sin_ref[...]
    seqs, _, _, blocks, pr, _ = kv_ref.shape
    for j in range(3):
        y = dot(normed, w_ref[j], 1, 0)
        for lo in range(0, y.shape[1], HEAD_DIM):
            cols = slice(lo, lo + HEAD_DIM)
            part = y[:, cols]
            if j < 2:
                part = part * cosine + pltpu.roll(part, HEAD_DIM // 2, 1) * sine
            part = part.astype(BF)
            if j == 0:
                q_ref[:, cols] = part
            else:
                for b in range(blocks):
                    for s in range(seqs):
                        at = (b * seqs + s) * pr
                        kv_ref[s, j - 1, 0, b, :, cols] = part[at : at + pr]


def project(rows, gain, weights, cosine, sine, seqs, n):
    count, width = rows.shape
    local = weights.shape[2]
    tile = 256
    pr = count // (2 * n * seqs)
    blocks = tile // (seqs * pr)
    per_span = n // blocks
    row = lambda w: pl.BlockSpec((tile, w), lambda i: (i, 0))
    return pl.pallas_call(
        project_kernel,
        grid=(count // tile,),
        in_specs=[
            row(width),
            pl.BlockSpec((1, width), lambda i: (0, 0)),
            pl.BlockSpec((3, width, local), lambda i: (0, 0, 0)),
            row(HEAD_DIM),
            row(HEAD_DIM),
        ],
        out_specs=[
            row(width),
            row(local),
            pl.BlockSpec(
                (seqs, 2, 1, blocks, pr, local),
                lambda i: (0, 0, i // per_span, lax.rem(i, per_span), 0, 0),
            ),
        ],
        out_shape=[
            jax.ShapeDtypeStruct((count, width), BF),
            jax.ShapeDtypeStruct((count, local), BF),
            jax.ShapeDtypeStruct((seqs, 2, 2, n, pr, local), BF),
        ],
        compiler_params=pltpu.CompilerParams(vmem_limit_bytes=40 * MIB),
        cost_estimate=pl.CostEstimate(
            flops=6 * count * width * local, bytes_accessed=4 * count * width, transcendentals=0
        ),
        name="project",
    )(rows, gain, weights, cosine, sine)


def relative(c, other, ctx_count):
    lanes = ctx_count // 2
    apart = lax.rem(c // 2 - other // 2 + lanes, lanes)
    return apart * 2 + lax.rem(c + other, 2)


def attend_kernel(ctx_count, c_ref, q_ref, k_ref, v_ref, fc_ref, fr_ref, *refs):
    o_ref, lse_ref = refs[-2:]
    c = c_ref[0]
    kind = pl.program_id(1)
    q = q_ref[...].reshape(k_ref.shape[3:])
    scale = HEAD_DIM**-0.5 * LOG2E

    def diag():
        s = dot(q, k_ref[0, 0, kind], 1, 1) * scale
        s = jnp.where(fr_ref[0] <= fc_ref[0], s, -1e30)
        m = jnp.max(s, axis=-1, keepdims=True)
        p = jnp.exp2(s - m)
        return m, jnp.sum(p, axis=-1, keepdims=True), dot(p.astype(BF), v_ref[0, 0, kind], 1, 0)

    def step(other, pp, state):
        m, l, acc = state
        j = relative(c, other, ctx_count)
        s = dot(q, k_ref[j, 0, pp], 1, 1) * scale
        m_new = jnp.maximum(m, jnp.max(s, axis=-1, keepdims=True))
        p = jnp.exp2(s - m_new)
        a = jnp.exp2(m - m_new)
        return (
            m_new,
            l * a + jnp.sum(p, axis=-1, keepdims=True),
            acc * a + dot(p.astype(BF), v_ref[j, 0, pp], 1, 0),
        )

    state = diag()
    state = lax.fori_loop(
        0, jnp.where(kind == 0, c, ctx_count), lambda i, st: step(i, 0, st), state
    )
    state = lax.fori_loop(
        jnp.where(kind == 0, ctx_count, c + 1), ctx_count, lambda i, st: step(i, 1, st), state
    )
    m, l, acc = state
    o_ref[...] = (acc / l).astype(BF).reshape(o_ref.shape)
    lse = jnp.broadcast_to(m + jnp.log2(l), acc.shape)
    lse_ref[0, 0] = jnp.transpose(lse)[:8]


def attend(c, q, kv, seq, flag_col, flag_row, out):
    ctx_count, _, _, span, local = kv.shape
    heads = local // HEAD_DIM
    _, n, _, pr, _ = q.shape
    block = (ctx_count, 1, 2, span, HEAD_DIM)
    ks = pl.BlockSpec(block, lambda h, t, c: (0, 0, 0, 0, h))
    vs = pl.BlockSpec(block, lambda h, t, c: (0, 1, 0, 0, h))
    qs = pl.BlockSpec((1, n, 1, pr, HEAD_DIM), lambda h, t, c: (t, 0, seq, 0, h))
    held = [] if out is None else [out]
    return pl.pallas_call(
        functools.partial(attend_kernel, ctx_count),
        grid_spec=pltpu.PrefetchScalarGridSpec(
            num_scalar_prefetch=1,
            grid=(heads, 2),
            in_specs=[
                qs,
                ks,
                vs,
                pl.BlockSpec((1, span, 1), lambda h, t, c: (t, 0, 0)),
                pl.BlockSpec((1, 1, span), lambda h, t, c: (t, 0, 0)),
            ]
            + [pl.BlockSpec(memory_space=pl.ANY)] * len(held),
            out_specs=[qs, pl.BlockSpec((1, 1, 8, span), lambda h, t, c: (h, t, 0, 0))],
        ),
        out_shape=[
            jax.ShapeDtypeStruct(q.shape, BF),
            jax.ShapeDtypeStruct((heads, 2, 8, span), F32),
        ],
        input_output_aliases={6: 0} if held else {},
        compiler_params=pltpu.CompilerParams(vmem_limit_bytes=48 * MIB),
        cost_estimate=pl.CostEstimate(
            flops=heads * 9 * 8 * span * span * HEAD_DIM, bytes_accessed=8 * MIB, transcendentals=0
        ),
        name="attend",
    )(c, q, kv, kv, flag_col, flag_row, *held)


def attend_back_kernel(
    ctx_count,
    c_ref,
    q_ref,
    k_ref,
    v_ref,
    do_ref,
    o_ref,
    lse_ref,
    cos_ref,
    sin_ref,
    fc_ref,
    fr_ref,
    *refs,
):
    dq_ref, dkv_ref, dk_acc, dv_acc, dq_acc = refs[-5:]
    flat = (k_ref.shape[3], k_ref.shape[4])
    c = c_ref[0]
    root = HEAD_DIM**-0.5
    dk_acc[...] = jnp.zeros_like(dk_acc)
    dv_acc[...] = jnp.zeros_like(dv_acc)
    for kind in range(2):
        q, do = q_ref[kind].reshape(flat), do_ref[kind].reshape(flat)
        product = do.astype(F32) * o_ref[kind].reshape(flat).astype(F32)
        delta = jnp.sum(jnp.transpose(product), axis=0, keepdims=True)
        lse = lse_ref[0, kind, 0:1]
        dq_acc[...] = jnp.zeros_like(dq_acc)

        def step(j, pp, masked, q=q, do=do, delta=delta, lse=lse, kind=kind):
            k, v = k_ref[j, 0, pp], v_ref[j, 0, pp]
            s = dot(k, q, 1, 1) * (root * LOG2E)
            if masked:
                s = jnp.where(fc_ref[kind] <= fr_ref[kind], s, -1e30)
            p = jnp.exp2(s - lse)
            dp = dot(v, do, 1, 1)
            ds = (p * (dp - delta)).astype(BF)
            dv_acc[j, pp] += dot(p.astype(BF), do, 1, 0)
            dk_acc[j, pp] += dot(ds, q, 1, 0)
            dq_acc[...] += dot(ds, k, 0, 0)

        step(0, kind, True)

        def plain(i, carry, pp):
            step(relative(c, i, ctx_count), pp, False)
            return carry

        if kind == 0:
            lax.fori_loop(0, c, functools.partial(plain, pp=0), 0)
        else:
            lax.fori_loop(0, ctx_count, functools.partial(plain, pp=0), 0)
            lax.fori_loop(c + 1, ctx_count, functools.partial(plain, pp=1), 0)
        dq = dq_acc[...] * root
        cosine, sine = cos_ref[kind].reshape(flat), sin_ref[kind].reshape(flat)
        dq = dq * cosine - pltpu.roll(dq, HEAD_DIM // 2, 1) * sine
        dq_ref[kind] = dq.astype(BF).reshape(dq_ref.shape[1:])
    dkv_ref[:, 0] = (dk_acc[...] * root).astype(BF)
    dkv_ref[:, 1] = dv_acc[...].astype(BF)


def attend_back(c, q, kv, do, o, lse, seq, cosine, sine, flag_col, flag_row, out, *deps):
    ctx_count, _, _, span, local = kv.shape
    heads = local // HEAD_DIM
    _, n, _, pr, _ = q.shape
    block = (ctx_count, 1, 2, span, HEAD_DIM)
    ks = pl.BlockSpec(block, lambda h, c: (0, 0, 0, 0, h))
    vs = pl.BlockSpec(block, lambda h, c: (0, 1, 0, 0, h))
    qs = pl.BlockSpec((2, n, 1, pr, HEAD_DIM), lambda h, c: (0, 0, seq, 0, h))
    table = pl.BlockSpec((2, n, 1, pr, HEAD_DIM), lambda h, c: (0, 0, seq, 0, 0))
    kv_out = pl.BlockSpec((ctx_count, 2, 2, span, HEAD_DIM), lambda h, c: (0, 0, 0, 0, h))
    held = ([] if out is None else [out]) + list(deps)
    return pl.pallas_call(
        functools.partial(attend_back_kernel, ctx_count),
        grid_spec=pltpu.PrefetchScalarGridSpec(
            num_scalar_prefetch=1,
            grid=(heads,),
            in_specs=[
                qs,
                ks,
                vs,
                qs,
                qs,
                pl.BlockSpec((1, 2, 8, span), lambda h, c: (h, 0, 0, 0)),
                table,
                table,
                pl.BlockSpec((2, span, 1), lambda h, c: (0, 0, 0)),
                pl.BlockSpec((2, 1, span), lambda h, c: (0, 0, 0)),
            ]
            + [pl.BlockSpec(memory_space=pl.ANY)] * len(held),
            out_specs=[qs, kv_out],
            scratch_shapes=[
                pltpu.VMEM((ctx_count, 2, span, HEAD_DIM), F32),
                pltpu.VMEM((ctx_count, 2, span, HEAD_DIM), F32),
                pltpu.VMEM((span, HEAD_DIM), F32),
            ],
        ),
        out_shape=[jax.ShapeDtypeStruct(q.shape, BF), jax.ShapeDtypeStruct(kv.shape, BF)],
        input_output_aliases={} if out is None else {11: 0},
        compiler_params=pltpu.CompilerParams(vmem_limit_bytes=56 * MIB),
        cost_estimate=pl.CostEstimate(
            flops=heads * 9 * 20 * span * span * HEAD_DIM, bytes_accessed=12 * MIB, transcendentals=0
        ),
        name="attend_back",
    )(c, q, kv, kv, do, o, lse, cosine, sine, flag_col, flag_row, *held)


def merge_kernel(n, ctx_count, c_ref, shard_ref, *refs):
    a_refs, b_refs, refs = refs[:n], refs[n : 2 * n], refs[2 * n :]
    pieces, refs = refs[:ctx_count], refs[ctx_count:]
    h_ref, gain_ref, r_ref, n_ref, own_ref, logit_ref, w_ref, mixed_ref, wide = refs
    i = pl.program_id(0)
    c = c_ref[0]
    count, local = wide.shape[0], wide.shape[1] // n
    own, tile, share = count // n, h_ref.shape[0], local // ctx_count
    per_span = count // tile

    @pl.when(i == 0)
    def _():
        half = ctx_count // 2
        for j in range(ctx_count):
            other = lax.rem(c // 2 - j // 2 + half, half) * 2 + lax.rem(c + j, 2)
            at = pl.multiple_of(other * share, share)
            for k in range(n):
                w_ref[k, pl.ds(at, share), :] = pieces[j][shard_ref[k]]

    def turned(ref, k, by):
        cols = slice(k * local, (k + 1) * local)
        wide[by * own :, cols] = ref[: count - by * own]
        if by:
            wide[: by * own, cols] = ref[count - by * own : count]

    @pl.when(i == 0)
    def _():
        for k in range(n):
            turned(a_refs[k], k, k)

    @pl.when(i == per_span)
    def _():
        for k in range(n):
            turned(b_refs[-k % n], k, -k % n)

    part = lax.rem(i, per_span)
    rows = wide[pl.ds(pl.multiple_of(part * tile, tile), tile), :]
    weights = w_ref[...].reshape(n * local, w_ref.shape[2])
    resid = h_ref[...].astype(F32) + dot(rows, weights, 1, 0)
    inverse = lax.rsqrt(jnp.mean(resid * resid, axis=-1, keepdims=True) + EPSILON)
    normed = (resid * inverse * gain_ref[...]).astype(BF)
    n_ref[...] = normed
    logit_ref[...] = dot(r_ref[...], normed, 1, 1)

    @pl.when(part == 0)
    def _():
        own_ref[0] = resid[:own]
        mixed_ref[0] = rows[:own]


def merge(c, shards, got_a, got_b, pieces, rows, gain, router_t):
    count, width = rows.shape
    n, ctx_count = len(got_a), len(pieces)
    span, local = got_b[0].shape
    tile = 256
    per_span, own = span // tile, span // n
    once = pl.Buffered(1)
    row = pl.BlockSpec((tile, width), lambda i, c, f: (i, 0))
    own_rows = pl.BlockSpec((1, own, width), lambda i, c, f: (i // per_span, 0, 0))
    whole = lambda shape: pl.BlockSpec(
        shape, lambda i, c, f: (0,) * len(shape), pipeline_mode=once
    )
    return pl.pallas_call(
        functools.partial(merge_kernel, n, ctx_count),
        grid_spec=pltpu.PrefetchScalarGridSpec(
            num_scalar_prefetch=2,
            grid=(count // tile,),
            in_specs=[whole((span, local))] * (2 * n)
            + [whole(pieces[0].shape)] * ctx_count
            + [row, whole((1, width)), whole(router_t.shape)],
            out_specs=[
                row,
                own_rows,
                pl.BlockSpec((router_t.shape[0], tile), lambda i, c, f: (0, i)),
                whole((n, local, width)),
                own_rows,
            ],
            scratch_shapes=[pltpu.VMEM((span, width), BF)],
        ),
        out_shape=[
            jax.ShapeDtypeStruct((count, width), BF),
            jax.ShapeDtypeStruct((count // span, own, width), F32),
            jax.ShapeDtypeStruct((router_t.shape[0], count), F32),
            jax.ShapeDtypeStruct((n, local, width), BF),
            jax.ShapeDtypeStruct((count // span, own, width), BF),
        ],
        compiler_params=pltpu.CompilerParams(vmem_limit_bytes=60 * MIB),
        cost_estimate=pl.CostEstimate(
            flops=2 * count * width * width, bytes_accessed=8 * count * width, transcendentals=0
        ),
        name="merge",
    )(c, shards, *got_a, *got_b, *pieces, rows, gain, router_t)


def project_back_kernel(seqs, dq_ref, *refs):
    pairs, refs = refs[:seqs], refs[seqs:]
    cos_ref, sin_ref, w_ref, h_ref, raw_ref, gn_ref, gain_ref = refs
    x = h_ref[...].astype(F32)
    inverse = lax.rsqrt(jnp.mean(x * x, axis=-1, keepdims=True) + EPSILON)
    cosine, sine = cos_ref[...], sin_ref[...]
    _, _, blocks, pr, local = pairs[0].shape
    raw_ref[0] = dq_ref[...]
    for b in range(blocks):
        for s in range(seqs):
            at = slice((b * seqs + s) * pr, (b * seqs + s + 1) * pr)
            raw_ref[2, at] = pairs[s][1, 0, b].astype(BF)
            for lo in range(0, local, HEAD_DIM):
                cols = slice(lo, lo + HEAD_DIM)
                part = pairs[s][0, 0, b, :, cols].astype(F32)
                part = part * cosine[at] - pltpu.roll(part, HEAD_DIM // 2, 1) * sine[at]
                raw_ref[1, at, cols] = part.astype(BF)
    gn = dot(raw_ref[0], w_ref[0], 1, 1)
    gn += dot(raw_ref[1], w_ref[1], 1, 1)
    gn += dot(raw_ref[2], w_ref[2], 1, 1)
    gn_ref[...] = gn.astype(BF)
    part = jnp.sum((gn * x * inverse).reshape(-1, 8, x.shape[1]), axis=0)

    @pl.when(pl.program_id(0) == 0)
    def _():
        gain_ref[...] = part

    @pl.when(pl.program_id(0) != 0)
    def _():
        gain_ref[...] += part


def project_back(dq, pairs, cosine, sine, weights, rows):
    count, width = rows.shape
    local = weights.shape[2]
    seqs = len(pairs)
    _, _, n, pr, _ = pairs[0].shape
    tile = 256
    blocks = tile // (seqs * pr)
    per_span = n // blocks
    row = lambda w: pl.BlockSpec((tile, w), lambda i: (i, 0))
    pair = pl.BlockSpec(
        (2, 1, blocks, pr, local), lambda i: (0, i // per_span, lax.rem(i, per_span), 0, 0)
    )
    return pl.pallas_call(
        functools.partial(project_back_kernel, seqs),
        grid=(count // tile,),
        in_specs=[row(local)]
        + [pair] * seqs
        + [
            row(HEAD_DIM),
            row(HEAD_DIM),
            pl.BlockSpec((3, width, local), lambda i: (0, 0, 0)),
            row(width),
        ],
        out_specs=[
            pl.BlockSpec((3, tile, local), lambda i: (0, i, 0)),
            row(width),
            pl.BlockSpec((8, width), lambda i: (0, 0)),
        ],
        out_shape=[
            jax.ShapeDtypeStruct((3, count, local), BF),
            jax.ShapeDtypeStruct((count, width), BF),
            jax.ShapeDtypeStruct((8, width), F32),
        ],
        compiler_params=pltpu.CompilerParams(vmem_limit_bytes=48 * MIB),
        cost_estimate=pl.CostEstimate(
            flops=6 * count * width * local, bytes_accessed=6 * count * width, transcendentals=0
        ),
        name="project_back",
    )(dq, *pairs, cosine, sine, weights, rows)


def spread(ref, rows):
    lead = ref.shape[:-2]
    if ref.shape[-2] % 16 == 0 or not lead:
        return [ref[...].reshape(rows, ref.shape[-1])]
    return [ref[index] for index in np.ndindex(*lead)]


def inner_kernel(expert_tiles, blocks, shard_ref, x_ref, *refs):
    c_refs, refs = refs[:blocks], refs[blocks:]
    mix_ref, ei_ref, si_ref, eo_ref, so_ref, d_ref, act_ref, dot_ref, c_all = refs
    k = pl.program_id(0)
    x_rows, c_rows = x_ref.shape[0], 256
    cut = c_refs[0].shape[2]

    @pl.when(k == 0)
    def _():
        for m in range(blocks):
            c_all[m * cut : (m + 1) * cut] = c_refs[m][0, 0]

    rows_in, rows_out = d_ref.shape[1], act_ref.shape[1]

    def finish(h_gate, h_up, u, scale):
        sig = 1.0 / (1.0 + jnp.exp(-h_gate))
        silu = h_gate * sig
        act = silu * h_up
        gu = u * scale
        d_gate = gu * h_up * sig * (1.0 + h_gate * (1.0 - sig))
        dots = jnp.sum(act * u, axis=0, keepdims=True)
        return (act * scale).astype(BF), d_gate.astype(BF), (gu * silu).astype(BF), dots

    def run(w_in, w_out, groups):
        size = rows_out // groups
        for lo in range(0, x_rows, c_rows):
            cols = slice(lo, lo + c_rows)
            xt, ct = x_ref[cols], c_all[cols]
            h = jnp.concatenate([dot(w, xt, 1, 1) for w in spread(w_in, rows_in)])
            u = jnp.concatenate([dot(w, ct, 1, 1) for w in spread(w_out, rows_out)])
            for g in range(groups):
                at = g * 2 * size
                act, dg, du, dots = finish(
                    h[at : at + size],
                    h[at + size : at + 2 * size],
                    u[g * size : (g + 1) * size],
                    mix_ref[0, g : g + 1, cols],
                )
                act_ref[0, g * size : (g + 1) * size, cols] = act
                d_ref[0, at : at + size, cols] = dg
                d_ref[0, at + size : at + 2 * size, cols] = du
                dot_ref[0, g : g + 1, cols] = dots

    @pl.when(k < expert_tiles)
    def _():
        run(ei_ref, eo_ref, 2)

    @pl.when(k >= expert_tiles)
    def _():
        run(si_ref, so_ref, 1)


def tile_specs(expert_in, shared_in, expert_out, shared_out, index, width):
    experts, _, f, _ = expert_in.shape
    last, share = experts // 2 - 1, 2 * f
    lo = lambda *i: jnp.minimum(index(*i), last)
    hi = lambda *i: jnp.maximum(index(*i) - last - 1, 0)
    return (
        pl.BlockSpec((2, 2, f, width), lambda *i: (lo(*i), 0, 0, 0)),
        pl.BlockSpec((2, share, width), lambda *i: (0, hi(*i), 0)),
        pl.BlockSpec((2, f, width), lambda *i: (lo(*i), 0, 0)),
        pl.BlockSpec((share, width), lambda *i: (hi(*i), 0)),
    )


def block_specs(n, cut, width):
    return [
        pl.BlockSpec(
            (1, 1, cut, width),
            lambda i, *p, t=t, k=k: (p[-1][t * n + k], t, 0, 0),
            pipeline_mode=pl.Buffered(1),
        )
        for t in range(2)
        for k in range(n)
    ]


def inner(shards, x, cot, mix, weights):
    rows, width = x.shape
    n, _, cut, _ = cot.shape
    expert_in, shared_in, expert_out, shared_out = weights
    f = expert_in.shape[2]
    tiles = expert_in.shape[0] // 2 + shared_out.shape[0] // (2 * f)
    whole = pl.BlockSpec((rows, width), lambda i, p: (0, 0), pipeline_mode=pl.Buffered(1))
    out = lambda r: pl.BlockSpec((1, r, rows), lambda i, p: (i, 0, 0))
    return pl.pallas_call(
        functools.partial(inner_kernel, expert_in.shape[0] // 2, 2 * n),
        grid_spec=pltpu.PrefetchScalarGridSpec(
            num_scalar_prefetch=1,
            grid=(tiles,),
            in_specs=[whole]
            + block_specs(n, cut, width)
            + [out(8), *tile_specs(*weights, lambda i, p: i, width)],
            out_specs=[out(4 * f), out(2 * f), out(8)],
            scratch_shapes=[pltpu.VMEM((rows, width), BF)],
        ),
        out_shape=[
            jax.ShapeDtypeStruct((tiles, 4 * f, rows), BF),
            jax.ShapeDtypeStruct((tiles, 2 * f, rows), BF),
            jax.ShapeDtypeStruct((tiles, 8, rows), F32),
        ],
        compiler_params=pltpu.CompilerParams(vmem_limit_bytes=62 * MIB),
        cost_estimate=pl.CostEstimate(
            flops=12 * f * rows * width * tiles,
            bytes_accessed=12 * f * width * tiles + 4 * rows * width,
            transcendentals=0,
        ),
        name="inner",
    )(shards, x, *[cot] * (2 * n), mix, *weights)


def outer_kernel(expert_tiles, shard_ref, d_ref, e_ref, s_ref, *refs):
    o_ref, acc = refs[-2:]
    k = pl.program_id(1)
    n, _, cut, _ = o_ref.shape

    @pl.when(k == 0)
    def _():
        acc[...] = jnp.zeros_like(acc)

    def run(w_ref):
        units = d_ref.shape[0] * d_ref.shape[1]
        hid = d_ref[...].reshape(units, d_ref.shape[2])
        at = 0
        for w in spread(w_ref, units):
            for lo in range(0, acc.shape[1], 512):
                acc[:, lo : lo + 512] += dot(
                    hid[at : at + w.shape[0]], w[:, lo : lo + 512], 0, 0
                )
            at += w.shape[0]

    @pl.when(k < expert_tiles)
    def _():
        run(e_ref)

    @pl.when(k >= expert_tiles)
    def _():
        run(s_ref)

    @pl.when(k == pl.num_programs(1) - 1)
    def _():
        first = pl.program_id(0) * n
        for m in range(n):
            to = m if shard_ref is None else shard_ref[first + m]
            o_ref[to, 0] = acc[m * cut : (m + 1) * cut].astype(BF)


def outer(shards, n, hid, expert, shared, *deps):
    tiles, units, tokens = hid.shape
    width, f = expert.shape[-1], expert.shape[-2]
    rows = tokens // 2
    if expert.ndim == 4:
        group, step = 1, 2
        e_shape, s_shape = (2, 2, f, width), (2, 2 * f, width)
    else:
        group, step = 2, 4
        e_shape, s_shape = (4, f, width), (4 * f, width)
    last = expert.shape[0] // step - 1
    lo = lambda k: jnp.minimum(k, last)
    hi = lambda k: jnp.maximum(k - last - 1, 0)
    if expert.ndim == 4:
        e_spec = pl.BlockSpec(e_shape, lambda t, k, *p: (lo(k), 0, 0, 0))
        s_spec = pl.BlockSpec(s_shape, lambda t, k, *p: (0, hi(k), 0))
    else:
        e_spec = pl.BlockSpec(e_shape, lambda t, k, *p: (lo(k), 0, 0))
        s_spec = pl.BlockSpec(s_shape, lambda t, k, *p: (hi(k), 0))
    return pl.pallas_call(
        functools.partial(outer_kernel, last + 1)
        if shards is not None
        else functools.partial(outer_kernel, last + 1, None),
        grid_spec=pltpu.PrefetchScalarGridSpec(
            num_scalar_prefetch=0 if shards is None else 1,
            grid=(2, tiles // group),
            in_specs=[pl.BlockSpec((group, units, rows), lambda t, k, *p: (k, 0, t)), e_spec, s_spec]
        + [pl.BlockSpec(memory_space=pl.ANY)] * len(deps),
            out_specs=pl.BlockSpec((n, 1, rows // n, width), lambda t, k, *p: (0, t, 0, 0)),
            scratch_shapes=[pltpu.VMEM((rows, width), F32)],
        ),
        out_shape=jax.ShapeDtypeStruct((n, 2, rows // n, width), BF),
        compiler_params=pltpu.CompilerParams(vmem_limit_bytes=58 * MIB),
        cost_estimate=pl.CostEstimate(
            flops=2 * tiles * units * tokens * width,
            bytes_accessed=2 * tiles * units * (tokens + 2 * width) + 2 * tokens * width,
            transcendentals=0,
        ),
        name="outer",
    )(*([] if shards is None else [shards]), hid, expert, shared, *deps)


def weight_kernel(blocks, core_ref, shard_ref, h_ref, *refs):
    o_ref = refs[-1]
    for lo in range(0, o_ref.shape[2], 512):
        cols = slice(lo, lo + 512)
        if blocks:
            other = jnp.concatenate([ref[0, 0, :, cols] for ref in refs[:blocks]])
        else:
            other = refs[0][:, cols]
        o_ref[0, :, cols] = dot(h_ref[0], other, 1, 0).astype(BF)


def weight_grad(core, shards, hid, other, base, stride, piece, pieces, *deps):
    _, units, tokens = hid.shape
    units = units // pieces
    width = other.shape[-1]
    if other.ndim == 4:
        specs = block_specs(other.shape[0], other.shape[2], width)
    else:
        specs = [
            pl.BlockSpec((tokens, width), lambda i, c, p: (0, 0), pipeline_mode=pl.Buffered(1))
        ]
    return pl.pallas_call(
        functools.partial(weight_kernel, len(specs) if other.ndim == 4 else 0),
        grid_spec=pltpu.PrefetchScalarGridSpec(
            num_scalar_prefetch=2,
            grid=(2,),
            in_specs=[
                pl.BlockSpec((1, units, tokens), lambda i, c, p: (base + stride * i, piece, 0)),
            ]
            + specs
            + [pl.BlockSpec(memory_space=pl.ANY)] * len(deps),
            out_specs=pl.BlockSpec(
                (1, units, width), lambda i, c, p: (lax.rem(i + c[0], 2), 0, 0)
            ),
        ),
        out_shape=jax.ShapeDtypeStruct((2, units, width), BF),
        compiler_params=pltpu.CompilerParams(vmem_limit_bytes=40 * MIB),
        cost_estimate=pl.CostEstimate(
            flops=4 * units * tokens * width,
            bytes_accessed=4 * units * (tokens + width) + 2 * tokens * width,
            transcendentals=0,
        ),
        name="weight_grad",
    )(core, shards, hid, *[other] * len(specs), *deps)


def finish_kernel(core_ref, *refs):
    o_ref = refs[-1]
    which = pl.program_id(0) * pl.num_programs(1) + pl.program_id(1)
    for m, ref in enumerate(refs[:-1]):

        @pl.when(which == m)
        def _(ref=ref):
            o_ref[...] = ref[...].astype(F32).reshape(o_ref.shape)


def finish(core, kept, got, gated):
    count = len(kept)
    rows, width = kept[0].shape
    tile = rows // 2 if rows % 32 == 0 else rows
    steps = rows // tile
    at = lambda m: lambda h, j, r, c: (
        jnp.where(h * count + j == m, r, jnp.where(h * count + j < m, 0, steps - 1)),
        0,
    )
    if gated:
        shape = (count, 2, rows, width)
        place = lambda h, j, r, c: (j, lax.rem(h + c[0], 2), r, 0)
    else:
        shape = (2, count, rows, width)
        place = lambda h, j, r, c: (lax.rem(h + c[0], 2), j, r, 0)
    return pl.pallas_call(
        finish_kernel,
        grid_spec=pltpu.PrefetchScalarGridSpec(
            num_scalar_prefetch=1,
            grid=(2, count, steps),
            in_specs=[pl.BlockSpec((tile, width), at(m)) for m in range(2 * count)],
            out_specs=pl.BlockSpec((1, 1, tile, width), place),
        ),
        out_shape=jax.ShapeDtypeStruct(shape, F32),
        compiler_params=pltpu.CompilerParams(vmem_limit_bytes=40 * MIB),
        cost_estimate=pl.CostEstimate(
            flops=0, bytes_accessed=12 * count * rows * width, transcendentals=0
        ),
        name="finish",
    )(core, *kept, *got)


class Ring:
    def __init__(self, count):
        self.count = count
        self.order = ring_order(count)
        self.place = np.argsort(np.array(self.order))

    def shift(self, value, by):
        n = self.count
        pairs = [(self.order[i], self.order[(i + by) % n]) for i in range(n)]
        return lax.ppermute(value, "fsdp", pairs)

    def gather(self, ahead, behind):
        a, b = [ahead], [behind]
        for _ in range(self.count - 1):
            a.append(self.shift(a[-1], 1))
            b.append(self.shift(b[-1], -1))
        return a, b

    def scatter(self, ahead, behind, work=()):
        n = self.count
        a, b = ahead(1), behind(1)
        held = []
        for k in range(2, n + 1):
            kind = BF if k < n else F32
            a = (self.shift(a, 1).astype(F32) + ahead(k % n).astype(F32)).astype(kind)
            b = (self.shift(b, -1).astype(F32) + behind(k % n).astype(F32)).astype(kind)
            if held:
                a, b = after(a, *held), after(b, *held)
            held = work(k, a, b) if work else []
        return a, b, held


def ctx_pairs(ctx_count, lanes, core):
    half = ctx_count // 2
    return [(x * 2 + k, ((x + lanes) % half) * 2 + (k ^ core)) for x in range(half) for k in range(2)]


def ctx_gather(value, ctx_count):
    got = []
    for lanes in range(ctx_count // 2):
        mine = value if lanes == 0 else lax.ppermute(value, "ctx", ctx_pairs(ctx_count, lanes, 0))
        got.append(mine)
        got.append(lax.ppermute(mine, "ctx", ctx_pairs(ctx_count, 0, 1)))
    return got


def ctx_scatter(parts, ctx_count):
    half = ctx_count // 2
    total = None
    for lanes in reversed(range(half)):
        other = lax.ppermute(parts[2 * lanes + 1], "ctx", ctx_pairs(ctx_count, 0, 1))
        s = parts[2 * lanes].astype(F32) + other.astype(F32)
        if lanes:
            s = lax.ppermute(s.astype(BF), "ctx", ctx_pairs(ctx_count, -lanes % half, 0)).astype(F32)
        total = s if total is None else total + s
    return total


class Sum:
    def __init__(self, value):
        self.value = value

    def reduce(self):
        flip = ctx_pairs(4, 0, 1)
        keep, send = self.value[0], self.value[1]
        self.part = (keep.astype(F32) + lax.ppermute(send, "ctx", flip).astype(F32)).astype(BF)
        return self.part

    def cross(self, *ties):
        part = after(self.part, *ties) if ties else self.part
        self.got = lax.ppermute(part, "ctx", ctx_pairs(4, 1, 0))
        return self.got

    def finish(self, *ties):
        got = after(self.got, *ties) if ties else self.got
        t = (self.part.astype(F32) + got.astype(F32)).astype(BF)
        return t, lax.ppermute(t, "ctx", ctx_pairs(4, 0, 1))


def kept_table(route_rows, keys, experts, capacity):
    index = jnp.arange(keys.shape[0], dtype=jnp.int32)
    before = (keys[None, :] < keys[:, None]) | (
        (keys[None, :] == keys[:, None]) & (index[None, :] < index[:, None])
    )
    named = jnp.any(
        route_rows[None, :, :] == jnp.arange(experts, dtype=jnp.int32)[:, None, None], axis=2
    )
    ahead = dot(named.astype(BF), before.astype(BF), 1, 1)
    return (named & (ahead < capacity)).astype(BF)


def per_device(
    hidden_in,
    cotangent,
    routes,
    priority,
    gain_attn,
    attention_input_weights,
    attention_output_weights,
    gain_ffn,
    router,
    shared_gate,
    shared_in,
    shared_out,
    expert_in,
    expert_out,
):
    n = lax.axis_size("fsdp")
    ctx_count = lax.axis_size("ctx")
    c = lax.axis_index("ctx")
    core = lax.rem(c, 2)
    ring = Ring(n)
    place = jnp.asarray(ring.place, jnp.int32)[lax.axis_index("fsdp")]
    seqs, _, _, pr, width = hidden_in.shape
    span = pr * n
    local = attention_input_weights.shape[2]
    experts = expert_in.shape[0]
    top = routes.shape[-1]
    own_rows = seqs * 2 * pr
    tokens = own_rows * n
    capacity = 5 * own_rows * top // (4 * experts)
    slices = width // n

    cut = seqs * pr
    hidden = jnp.transpose(hidden_in[:, :, 0], (1, 0, 2, 3)).reshape(2, cut, width)

    def as_rows(value):
        value = value.reshape(-1)
        return jnp.pad(value, (0, 8 * width - value.size)).reshape(8, width)

    small = jnp.concatenate([gain_attn[None], gain_ffn[None], shared_gate[None], router.T])
    small_count = small.shape[0]
    got_a, got_b = ring.gather(jnp.concatenate([hidden[0], as_rows(small)]), hidden[1])
    last = got_a[-1], got_b[-1]
    places = jnp.asarray(ring.place, jnp.int32)
    order = jnp.asarray(ring.order, jnp.int32)
    steps = jnp.arange(n, dtype=jnp.int32)
    place = after(place, got_a[2])
    by_shard = (place - places) % n
    shards = jnp.stack([order[(place - steps) % n], order[(place + steps) % n]])
    offset = shards[:, :, None] * pr + jnp.arange(pr, dtype=jnp.int32)
    c_later = after(c, got_a[3])
    start = jnp.stack([c_later, 2 * ctx_count - 1 - c_later]) * span
    positions = start[:, None, None] + offset
    flags = (offset // BLOCK).astype(F32).reshape(2, span)
    flag_col, flag_row = flags[:, :, None], flags[:, None, :]
    halves = jnp.arange(HEAD_DIM, dtype=jnp.int32) % (HEAD_DIM // 2)
    frequency = ROPE_BASE ** (-2.0 * halves.astype(F32) / HEAD_DIM)
    angles = positions.astype(F32)[..., None] * frequency
    sign = jnp.where(jnp.arange(HEAD_DIM) < HEAD_DIM // 2, -1.0, 1.0)
    by_seq = (2, n, seqs, pr, HEAD_DIM)
    cosine = jnp.broadcast_to(jnp.cos(angles)[:, :, None], by_seq)
    sine = jnp.broadcast_to((jnp.sin(angles) * sign)[:, :, None], by_seq)
    flat_cos, flat_sin = cosine.reshape(tokens, HEAD_DIM), sine.reshape(tokens, HEAD_DIM)

    shard_list = shards.reshape(-1)
    c_arr = c.reshape(1).astype(jnp.int32)
    core_arr = core.reshape(1).astype(jnp.int32)
    smalls = jnp.stack([g[cut:].reshape(-1)[: small.size] for g in got_a])
    smalls = smalls.reshape(n, small_count, slices)
    smalls = jnp.take(smalls, by_shard, axis=0)
    smalls = jnp.transpose(smalls, (1, 0, 2)).reshape(small_count, width)
    all_rows = jnp.concatenate([g[:cut] for g in got_a] + got_b)
    gain_one, gain_two = smalls[0:1].astype(F32), smalls[1:2].astype(F32)
    logit_rows = jnp.concatenate(
        [smalls[3:], smalls[2:3], jnp.zeros((16 - experts - 1, width), BF)]
    )

    share = local // ctx_count
    mine = lax.dynamic_slice_in_dim(attention_output_weights, c * share, share, 0)
    out_piece = lax.all_gather(mine, "fsdp", axis=0)
    out_pieces = ctx_gather(out_piece, ctx_count)
    cot = jnp.transpose(cotangent[:, :, 0], (1, 0, 2, 3)).reshape(2, cut, width)
    cot_all = lax.all_gather(after(cot, got_a[n - 3]), "fsdp", axis=0)
    routes_in, priority_in = after(routes, got_a[5]), after(priority, got_a[5])
    kept_own = kept_table(
        routes_in.reshape(own_rows, top), priority_in.reshape(own_rows), experts, capacity
    )
    kept_fill = -(-kept_own.size // local) % 8
    kept_rows = jnp.pad(kept_own.reshape(-1, local), ((0, kept_fill and 8 - kept_fill), (0, 0)))

    normed_one, query, kv_own = project(
        all_rows, gain_one, attention_input_weights, flat_cos, flat_sin, seqs, n
    )
    query = query.reshape(2, n, seqs, pr, local)
    kvs = []
    for s in range(seqs):
        pieces = ctx_gather(kv_own[s], ctx_count)
        kvs.append(jnp.stack(pieces).reshape(ctx_count, 2, 2, span, local))

    mixed, log_sums = None, []
    for s in range(seqs):
        mixed, lse = attend(c_arr, query, kvs[s], s, flag_col, flag_row, mixed)
        log_sums.append(lse)
    sent = mixed.reshape(2, tokens // 2, local)
    got_a, got_b = ring.gather(jnp.concatenate([sent[0], kept_rows]), sent[1])
    kept = [
        g[tokens // 2 :].reshape(-1)[: kept_own.size].reshape(experts, seqs, 2, pr) for g in got_a
    ]
    kept = jnp.stack(
        [
            jnp.stack([g[:, :, 0] for g in kept], axis=1),
            jnp.stack([kept[(n - k) % n][:, :, 1] for k in range(n)], axis=1),
        ],
        axis=1,
    )
    kept = kept.reshape(experts, tokens).astype(F32)
    x, resid, logit, out_full, mixed_own = merge(
        c_arr, shard_list, got_a, got_b, out_pieces, all_rows, gain_two, logit_rows
    )
    out_full = out_full.reshape(width, width)
    resid = resid.reshape(own_rows, width)

    top_logit = jnp.max(logit[:experts], axis=0, keepdims=True)
    raised = jnp.exp(logit[:experts] - top_logit)
    gates = raised / jnp.sum(raised, axis=0, keepdims=True)
    weight_s = jax.nn.sigmoid(logit[experts : experts + 1])
    small_tiles = shared_out.shape[0] // (2 * expert_in.shape[2])
    mix = jnp.concatenate(
        [
            jnp.pad((gates * kept).reshape(experts // 2, 2, tokens), ((0, 0), (0, 6), (0, 0))),
            jnp.broadcast_to(jnp.pad(weight_s, ((0, 7), (0, 0)))[None], (small_tiles, 8, tokens)),
        ]
    )
    d_buf, act_buf, dots = inner(
        shard_list, x, cot_all, mix, (expert_in, shared_in, expert_out, shared_out)
    )
    split = lambda value: value.reshape(2, n, cut, width)
    dots_e = dots[: experts // 2, :2].reshape(experts, tokens) * kept
    dots_s = jnp.sum(dots[experts // 2 :, 0], axis=0, keepdims=True)
    dots = jnp.concatenate([dots_e, dots_s, jnp.zeros((7, tokens), F32)])
    dots = dots.reshape(16, 2, n, cut)
    dots = jnp.stack(
        [jnp.take(dots[:, 0], by_shard, axis=1), jnp.take(dots[:, 1], -by_shard % n, axis=1)],
        axis=2,
    )
    dots = jnp.transpose(dots, (1, 0, 2, 3)).reshape(n, 16, own_rows)
    dot_own = lax.psum_scatter(dots, "fsdp", scatter_dimension=0, tiled=True)[0]

    f = expert_in.shape[2]
    quarter = experts // 4
    halves = small_tiles // 2
    four = ctx_count == 4
    spots = [(j, quarter) for j in range(quarter)] + [
        (experts // 2 + j, halves) for j in range(halves)
    ]
    sums = {}

    def weight_piece(key, *ties):
        name, base, piece = key
        buf, other = (d_buf, x) if name == "in" else (act_buf, cot_all)
        sums[key] = Sum(
            weight_grad(
                core_arr,
                shard_list,
                buf,
                other,
                base,
                dict(spots)[base],
                piece,
                2 if name == "in" else 1,
                *ties,
            )
        )
        return sums[key].value

    late = [("out", base, 0) for base, _ in spots]
    queue = [("in", base, piece) for base, _ in spots for piece in (0, 1)]
    flown = []

    def fly(key):
        if four:
            sums[key].reduce()
            flown.append(sums[key].cross(*flown[-2:-1]))
            return [flown[-1]]
        return []

    early = []
    for key in late[:2]:
        early.append(weight_piece(key))
    early_got = [fly(key) for key in late[:2]]
    if four:
        early = [sums[key].part for key in late[:2]]
    grad_in = outer(None, n, d_buf, expert_in, shared_in, *early)

    def beside(k, a, b):
        held = []
        if k - 2 < len(queue):
            held.append(weight_piece(queue[k - 2], a, b))
        if four and 0 <= k - 3 < len(queue):
            held.append(sums[queue[k - 3]].reduce())
            flown.append(sums[queue[k - 3]].cross(*flown[-2:-1]))
        if k in (3, 5):
            held += early_got[(k - 3) // 2]
        if k == n - 1 and four:
            held.append(sums[queue[0]].got)
        return held

    gi_a, gi_b, _ = ring.scatter(lambda k: grad_in[k, 0], lambda k: grad_in[k, 1], beside)
    for key in queue[n - 1 :]:
        weight_piece(key, gi_a, gi_b)
    if four:
        for key in queue[n - 2 :]:
            sums[key].reduce()
            flown.append(sums[key].cross(*flown[-2:-1]))
    got_in = [sums[key].got for key in queue] if four else []

    def norm_back(grad, value, gain):
        inverse = lax.rsqrt(jnp.mean(value * value, axis=-1, keepdims=True) + EPSILON)
        scaled = grad * gain
        return inverse * (
            scaled - value * inverse * inverse * jnp.mean(scaled * value, axis=-1, keepdims=True)
        ), inverse

    own_of = lambda value: value.reshape(-1, 2, n, cut)[:, :, 0].reshape(-1, own_rows)
    gates_own, weight_own = own_of(gates), own_of(weight_s)
    x_own = split(x)[:, 0].reshape(own_rows, width)
    d_gates = dot_own[:experts]
    d_logit = (
        gates_own * (d_gates - jnp.sum(gates_own * d_gates, axis=0, keepdims=True))
    ).astype(BF)
    d_gate_s = dot_own[experts : experts + 1] * weight_own * (1.0 - weight_own)
    d_rows = jnp.concatenate([d_gate_s, d_logit.astype(F32)])
    grad_n2 = jnp.concatenate([gi_a, gi_b])
    grad_n2 = grad_n2 + jnp.einsum("er,ed->rd", d_rows, smalls[2:].astype(F32), precision=EXACT)
    grad_small = jnp.einsum("er,rd->ed", d_rows, x_own.astype(F32), precision=EXACT)
    back, inverse_two = norm_back(grad_n2, resid, gain_two)
    grad_gain_two = jnp.sum(grad_n2 * resid * inverse_two, axis=0, keepdims=True)
    grad_mid = cot.reshape(own_rows, width).astype(F32) + back
    branch = grad_mid.astype(BF)

    grad_mixed = dot(branch, out_full, 1, 1).astype(BF)
    grad_mixed = jnp.take(grad_mixed.reshape(own_rows, n, local), by_shard, axis=1)
    grad_mixed = jnp.transpose(grad_mixed, (1, 0, 2))
    out_part = outer(shard_list, n, act_buf, expert_out, shared_out, grad_mixed, *got_in[1:2])
    moved = lax.all_to_all(
        grad_mixed, "fsdp", split_axis=0, concat_axis=0, tiled=True
    ).reshape(n, 2, cut, local)
    d_o = jnp.concatenate(
        [jnp.take(moved[:, 0], shards[0], axis=0), jnp.take(moved[:, 1], shards[1], axis=0)]
    ).reshape(2, n, seqs, pr, local)
    d_o = after(d_o, out_part)

    in_place = lambda value: jnp.transpose(
        value.reshape(2, seqs, pr, width), (1, 0, 2, 3)
    ).reshape(hidden_in.shape)
    out_own = lax.psum_scatter(out_part, "fsdp", scatter_dimension=0, tiled=True)

    d_q, pairs = None, []
    for s in range(seqs):
        d_q, pair = attend_back(
            c_arr,
            query,
            kvs[s],
            d_o,
            mixed,
            log_sums[s],
            s,
            cosine,
            sine,
            flag_col,
            flag_row,
            d_q,
            *got_in[2 + s : 3 + s],
        )
        pair = ctx_scatter([pair[j] for j in range(ctx_count)], ctx_count)
        pairs.append(pair.astype(BF).reshape(2, 2, n, pr, local))
    d_q = after(d_q, out_own, *got_in[4:5])

    grad_out_own = dot(mixed_own.reshape(own_rows, width), branch, 0, 0).astype(BF)
    if four:
        flip, cross = ctx_pairs(4, 0, 1), ctx_pairs(4, 1, 0)
        lane = c // 2
        pick = lambda value, i, axis: lax.dynamic_index_in_dim(value, i, axis, keepdims=False)
        by_core = grad_out_own.reshape(n, 2, 2, share, width)
        part = pick(by_core, core, 2).astype(F32)
        part = part + lax.ppermute(pick(by_core, 1 - core, 2), "ctx", flip).astype(F32)
        part = part.astype(BF)
        quart_got = lax.ppermute(after(pick(part, 1 - lane, 1), *pairs), "ctx", cross)
    else:
        quart_got = lax.psum(grad_out_own, "ctx").reshape(n, local, width)

    raw, grad_n1, gain_part = project_back(
        d_q.reshape(tokens, local), pairs, flat_cos, flat_sin, attention_input_weights, all_rows
    )
    quart_got = after(quart_got, raw)
    quart = (pick(part, lane, 1).astype(F32) + quart_got.astype(F32)).astype(BF) if four else quart_got
    quart = jnp.take(quart, by_shard, axis=0)
    own_quart = lax.psum_scatter(quart, "fsdp", scatter_dimension=0, tiled=True)[0]

    grad_n1 = split(grad_n1)
    grad_gain_one = jnp.sum(gain_part, axis=0, keepdims=True)
    smalls_back = jnp.concatenate(
        [grad_gain_one, grad_gain_two, grad_small, jnp.zeros((16 - small_count, width), F32)]
    )
    smalls_back = jnp.transpose(smalls_back.reshape(16, n, slices), (1, 0, 2))
    small_own = lax.psum_scatter(smalls_back, "fsdp", scatter_dimension=0, tiled=True)[0]

    def beside_last(k, a, b):
        held = []
        if k == 2:
            held += [weight_piece(key, a, b) for key in late[2:]]
        if k == 3 and four:
            held += got_in[5:6]
            for key in late[2:]:
                sums[key].reduce()
                sums[key].cross(quart_got)
        if k == 5 and four:
            held.append(quart_got)
        if k == n - 1 and four:
            held += [sums[key].got for key in late[2:]]
        return held

    gn_a, gn_b, _ = ring.scatter(lambda k: grad_n1[0, k], lambda k: grad_n1[1, k], beside_last)
    back_one, _ = norm_back(
        jnp.concatenate([gn_a, gn_b]), hidden.reshape(own_rows, width).astype(F32), gain_one
    )
    grad_hidden = in_place((grad_mid + back_one).astype(BF))
    out_own = after(out_own, gn_a, gn_b).reshape(own_rows, width).astype(F32)
    layer_out = in_place((resid + out_own).astype(BF))
    small_own = after(small_own, gn_a, gn_b)
    if ctx_count == 4:
        small_own = small_own + lax.ppermute(small_own, "ctx", ctx_pairs(4, 0, 1))
        small_own = small_own + lax.ppermute(small_own, "ctx", ctx_pairs(4, 1, 0))
    else:
        small_own = lax.psum(small_own, "ctx")

    grad_attn_in = jnp.einsum("nd,jne->dje", normed_one, raw, preferred_element_type=F32)

    own_quart = after(own_quart, gn_a, gn_b)
    if ctx_count == 4:
        t = own_quart
        o = lax.ppermute(t, "ctx", cross)
        t = jnp.stack([jnp.where(lane == 0, t, o), jnp.where(lane == 0, o, t)])
        o = lax.ppermute(t, "ctx", flip)
        total_attn_out = jnp.stack(
            [jnp.where(core == 0, t, o), jnp.where(core == 0, o, t)], axis=1
        ).astype(F32)
    else:
        total_attn_out = own_quart.astype(F32)

    lo = range(quarter)
    hi = range(experts // 2, experts // 2 + halves)
    if four:
        done = {
            key: value.finish(*([raw] if key in queue[:4] else [gn_a, gn_b]))
            for key, value in sums.items()
        }

        def finished(keys, gated):
            kept_halves, got_halves = zip(*[done[key] for key in keys])
            return finish(core_arr, kept_halves, got_halves, gated)

        def halved(value):
            keep = lax.dynamic_index_in_dim(value, core, 0, keepdims=False)
            send = lax.dynamic_index_in_dim(value, 1 - core, 0, keepdims=False)
            one = Sum((keep.astype(BF), send.astype(BF)))
            one.reduce()
            one.cross(*([sums[key].got for key in late[2:]]))
            t, o = one.finish(gn_a, gn_b)
            return jnp.stack([jnp.where(core == 0, t, o), jnp.where(core == 0, o, t)]).astype(F32)

        total_expert_in = finished([("in", j, p) for j in lo for p in (0, 1)], False)
        total_expert_out = finished([("out", j, 0) for j in lo], False)
        total_shared_in = finished([("in", j, p) for j in hi for p in (0, 1)], True)
        total_shared_out = finished([("out", j, 0) for j in hi], False)
        total_attn_in = halved(grad_attn_in.reshape(2, width // 2, 3, local))
    else:
        first = core == 0

        def summed(keys, axis):
            values = [
                jnp.where(first, sums[key].value, jnp.flip(sums[key].value, axis=0))
                for key in keys
            ]
            return lax.psum(jnp.stack(values, axis=axis), "ctx").astype(F32)

        total_expert_in = summed([("in", j, p) for j in lo for p in (0, 1)], 1)
        total_expert_out = summed([("out", j, 0) for j in lo], 1)
        total_shared_in = summed([("in", j, p) for j in hi for p in (0, 1)], 0)
        total_shared_out = summed([("out", j, 0) for j in hi], 1)
        total_attn_in = lax.psum(grad_attn_in.astype(BF), "ctx").astype(F32)

    return (
        layer_out,
        grad_hidden,
        small_own[0],
        jnp.transpose(total_attn_in.reshape(width, 3, local), (1, 0, 2)),
        total_attn_out.reshape(local, width),
        small_own[1],
        small_own[3:small_count].T,
        small_own[2],
        total_shared_in.reshape(shared_in.shape),
        total_shared_out.reshape(shared_out.shape),
        total_expert_in.reshape(expert_in.shape),
        total_expert_out.reshape(expert_out.shape),
    )


def solution(mesh):
    rows = P(None, None, "ctx", "fsdp", None)
    return jax.shard_map(
        per_device,
        mesh=mesh,
        in_specs=(
            rows,
            rows,
            rows,
            P(None, None, "ctx", "fsdp"),
            P("fsdp"),
            P(None, None, "fsdp"),
            P("fsdp", None),
            P("fsdp"),
            P("fsdp", None),
            P("fsdp"),
            P(None, "fsdp", None),
            P("fsdp", None),
            P(None, None, "fsdp", None),
            P(None, "fsdp", None),
        ),
        out_specs=(
            rows,
            rows,
            P("fsdp"),
            P(None, None, "fsdp"),
            P("fsdp", None),
            P("fsdp"),
            P("fsdp", None),
            P("fsdp"),
            P(None, "fsdp", None),
            P("fsdp", None),
            P(None, None, "fsdp", None),
            P(None, "fsdp", None),
        ),
        check_vma=False,
    )
```

time: 5610 us -> 1180 us (0.21)
  waiting for transfers between devices: 4340 us -> 412 us
  matrix products: 664 us -> 23.9 us
  Pallas kernels: 0 us -> 402 us
  blocking collectives: 134 us -> 0 us
  other arithmetic: 255 us -> 127 us
  starting transfers between devices: 1.53 us -> 86.7 us
  local copies, waits for them, and re-layouts: 186 us -> 107 us
    reduce_scatter x7 -> x4, waiting for transfers between devices: 1900 us -> 28.5 us  [the longest x1 27.5 us: per_device(): lax.psum_scatter(quart, 'fsdp', scatter_dimension=0, tiled=True)[0]]
    all_gather x7 -> x2, waiting for transfers between devices: 1870 us -> 0.02 us  [the longest x1 0.01 us: per_device(): out_piece = lax.all_gather(mine, 'fsdp', axis=0)]
    dot_general x50 -> x6, matrix products: 664 us -> 23.9 us  [the longest x1 11.5 us: per_device(): jnp.einsum('nd,jne->dje', normed_one, raw, preferred_element_type=F32)]
    psum x1 -> x0, waiting for transfers between devices: 464 us -> none  [per_device(): lax.psum(grad_attn_in.astype(jnp.bfloat16), 'ctx').astype(jnp.float32)]
    pallas_call x0 -> x23, Pallas kernels: none -> 402 us  [the longest x2 78.9 us: outer(): pl.pallas_call(functools.partial(outer_kernel, last + 1) if shards is not...]
    ppermute x0 -> x107, waiting for transfers between devices: none -> 343 us  [the longest x56 243 us: shift(): return lax.ppermute(value, 'fsdp', pairs)]
    unnamed x17 -> x6, waiting for transfers between devices: 114 us -> 0.1 us
    all_gather x4 -> x0, blocking collectives: 92.9 us -> none  [the longest x1 31.9 us: per_device(): lax.all_gather(router, 'fsdp', axis=0, tiled=True)]
  transfers between devices with their start and end apart: 16 -> 114, of which waited for: 16 -> 47; matrix products, arithmetic and copies ran while one was open for 8% -> 20% of each run, Pallas kernels for 0% -> 24%
where the time goes in v1:
time: 1180 us; the launch traced here: 1170 us
  waiting for transfers between devices  412 us (35%)
  Pallas kernels  402 us (34%)
  other arithmetic  127 us (11%)
  local copies, waits for them, and re-layouts  107 us (9%)
  starting transfers between devices  86.7 us (7%)
  matrix products  23.9 us (2%)
  between operations  16.4 us (1%)
    ppermute x56, waiting for transfers between devices, shift(): return lax.ppermute(value, 'fsdp', pairs)  243 us
    pallas_call x2, Pallas kernels, outer(): pl.pallas_call(functools.partial(outer_kernel, last + 1) if shards is not...  78.9 us
    pallas_call x9, Pallas kernels, weight_grad(): pl.pallas_call(functools.partial(weight_kernel, len(specs) if other.ndim...  75.1 us
    pallas_call x1, Pallas kernels, inner(): pl.pallas_call(functools.partial(inner_kernel, expert_in.shape[0] // 2, 2...  73.5 us
    ppermute x56, starting transfers between devices, shift(): return lax.ppermute(value, 'fsdp', pairs)  55.7 us
    pallas_call x2, Pallas kernels, attend_back(): pl.pallas_call(functools.partial(attend_back_kernel, ctx_count), grid_spe...  42.3 us
    all_to_all x1, waiting for transfers between devices, per_device(): lax.all_to_all(grad_mixed, 'fsdp', split_axis=0, concat_axis=0, tiled=True)  40 us
    pallas_call x1, Pallas kernels, merge(): pl.pallas_call(functools.partial(merge_kernel, n, ctx_count), grid_spec=p...  39.5 us
  transfers between devices with their start and end apart: 114, of which 47 were waited for; matrix products, arithmetic and copies ran while one was open for 20% of the time, Pallas kernels for 24%

profile of v1, /device:TPU:0, one launch (start us, length us, event | category | flops | bytes accessed | tf_op | source)
XLA Modules:
  0.0 1173.9 jit_solution(8963349530680070855)
XLA Ops:
  31.0 16.6 %collective-permute-done.8 = bf16[128,2048]{1,0:T(8,128)(2,1)S(1)} collective-permute-done((bf16[128,2048]{1,0:T(8,128)(2,1)}, bf16[128,2048]{1,0:T(8,128)(2,1)S(1)}, u32[]{:S(2)}, u32[]{:S(2)}) %collective-permute-start.8) | collective-permute-done | bytes 524320 | tf_op jit(solution)/shard_map/ppermute | solution.py:754
  54.5 22.7 %collective-permute-done.9 = bf16[128,2048]{1,0:T(8,128)(2,1)} collective-permute-done((bf16[128,2048]{1,0:T(8,128)(2,1)S(1)}, bf16[128,2048]{1,0:T(8,128)(2,1)}, u32[]{:S(2)}, u32[]{:S(2)}) %collective-permute-start.9) | collective-permute-done | bytes 524320 | tf_op jit(solution)/shard_map/ppermute | solution.py:754
  150.0 13.7 %project.1 = (bf16[2048,2048]{1,0:T(8,128)(2,1)}, bf16[2048,256]{1,0:T(8,128)(2,1)S(1)}, bf16[2,2,2,8,64,256]{5,4,3,2,1,0:T(8,128)(2,1)S(1)}) custom-call(bf16[2048,2048]{1,0:T(8,128)(2,1)} %constant_dynamic-update-slice_fusion.h_ref.refs_20_.refs_5_, f32[1,2048]{1,0:T(1,128)S(1)} %bitcast.643, bf16[3,2048,256]{2,1,0:T(8,128)(2,1)S(1)} %copy-done.24, ...), custom_call_target="tpu_custom_call" | custom-call | flops 6442450944 | bytes 16777216 | tf_op jit(solution)/shard_map/project/pallas_call | solution.py:75
  171.1 20.9 %collective-permute-done.15 = bf16[2,2,8,64,256]{4,3,2,1,0:T(8,128)(2,1)} collective-permute-done((bf16[2,2,8,64,256]{4,3,2,1,0:T(8,128)(2,1)}, bf16[2,2,8,64,256]{4,3,2,1,0:T(8,128)(2,1)}, u32[]{:S(2)}, u32[]{:S(2)}) %collective-permute-start.15) | collective-permute-done | bytes 1048608 | tf_op jit(solution)/shard_map/ppermute | solution.py:785
  195.2 15.0 %collective-permute-done.18 = bf16[2,2,8,64,256]{4,3,2,1,0:T(8,128)(2,1)} collective-permute-done((bf16[2,2,8,64,256]{4,3,2,1,0:T(8,128)(2,1)}, bf16[2,2,8,64,256]{4,3,2,1,0:T(8,128)(2,1)}, u32[]{:S(2)}, u32[]{:S(2)}) %collective-permute-start.18) | collective-permute-done | bytes 1048608 | tf_op jit(solution)/shard_map/ppermute | solution.py:785
  220.3 15.8 %attend.2 = (bf16[2,8,2,64,256]{4,3,2,1,0:T(8,128)(2,1)S(1)}, f32[2,2,8,512]{3,2,1,0:T(8,128)S(1)}) custom-call(s32[1]{0:T(128)} %bitcast.c_ref, bf16[2,8,2,64,256]{4,3,2,1,0:T(8,128)(2,1)S(1)} %bitcast.646, bf16[4,2,2,512,256]{4,3,2,1,0:T(8,128)(2,1)} %pad_maximum_fusion.1.k_ref.v_ref, bf16[4,2,2,512,256]{4,3,2,1,0:T(8,128)(2,1)} %pad_maximum_fusion.1.k_ref.v_ref, ...), custom_call_target="tpu_custom_call" | custom-call | flops 4831838208 | bytes 8388608 | tf_op jit(solution)/shard_map/attend/pallas_call | solution.py:161
  236.7 15.8 %attend.3 = (bf16[2,8,2,64,256]{4,3,2,1,0:T(8,128)(2,1)S(1)}, f32[2,2,8,512]{3,2,1,0:T(8,128)S(1)}) custom-call(s32[1]{0:T(128)} %bitcast.c_ref, bf16[2,8,2,64,256]{4,3,2,1,0:T(8,128)(2,1)S(1)} %bitcast.647, bf16[4,2,2,512,256]{4,3,2,1,0:T(8,128)(2,1)} %pad_maximum_fusion.k_ref.v_ref, ...), custom_call_target="tpu_custom_call", output_to_operand_aliasing={{0}: (6, {})} | custom-call | flops 4831838208 | bytes 8388608 | tf_op jit(solution)/shard_map/attend/pallas_call | solution.py:161
  259.2 30.0 %collective-permute-done.27.refs_9_ = bf16[1024,256]{1,0:T(8,128)(2,1)} collective-permute-done((bf16[1024,256]{1,0:T(8,128)(2,1)S(1)}, bf16[1024,256]{1,0:T(8,128)(2,1)}, u32[]{:S(2)}, u32[]{:S(2)}) %collective-permute-start.27) | collective-permute-done | bytes 524320 | tf_op jit(solution)/shard_map/ppermute | solution.py:754
  291.6 17.2 %collective-permute-done.28.refs_10_ = bf16[1024,256]{1,0:T(8,128)(2,1)} collective-permute-done((bf16[1024,256]{1,0:T(8,128)(2,1)}, bf16[1024,256]{1,0:T(8,128)(2,1)}, u32[]{:S(2)}, u32[]{:S(2)}) %collective-permute-start.28) | collective-permute-done | bytes 524320 | tf_op jit(solution)/shard_map/ppermute | solution.py:754
  311.2 11.7 collective-permute-done.29.refs_11_
  375.5 39.5 %merge.1 = (bf16[2048,2048]{1,0:T(8,128)(2,1)}, f32[2,128,2048]{2,1,0:T(8,128)}, f32[16,2048]{1,0:T(8,128)}, bf16[8,256,2048]{2,1,0:T(8,128)(2,1)}, bf16[2,128,2048]{2,1,0:T(8,128)(2,1)}) custom-call(s32[1]{0:T(128)} %bitcast.c_ref, s32[16]{0:T(128)} %reshape.840.shard_ref, bf16[1032,256]{1,0:T(8,128)(2,1)} %copy-done.55, bf16[1032,256]{1,0:T(8,128)(2,1)} %copy-done.79, ...), custom_call_target="tpu_custom_call" | custom-call | flops 17179869184 | bytes 33554432 | tf_op jit(solution)/shard_map/merge/pallas_call | solution.py:356
  422.6 73.5 %inner.1 = (bf16[6,704,2048]{2,1,0:T(8,128)(2,1)}, bf16[6,352,2048]{2,1,0:T(8,128)(2,1)}, f32[6,8,2048]{2,1,0:T(8,128)}) custom-call(s32[16]{0:T(128)} %reshape.840.shard_ref, bf16[2048,2048]{1,0:T(8,128)(2,1)} %get-tuple-element.95.x_ref.refs_0_, bf16[8,2,128,2048]{3,2,1,0:T(8,128)(2,1)} %bitcast.570, bf16[8,2,128,2048]{3,2,1,0:T(8,128)(2,1)} %bitcast.571, ...), custom_call_target="tpu_custom_call" | custom-call | flops 53150220288 | bytes 42729472 | tf_op jit(solution)/shard_map/inner/pallas_call | solution.py:553
  530.3 49.6 %outer.2 = bf16[8,2,128,2048]{3,2,1,0:T(8,128)(2,1)} custom-call(bf16[6,704,2048]{2,1,0:T(8,128)(2,1)} %get-tuple-element.99.d_ref.h_ref, bf16[8,2,176,2048]{3,2,1,0:T(8,128)(2,1)} %e_ref.2, bf16[2,704,2048]{2,1,0:T(8,128)(2,1)} %s_ref.2, bf16[352,2048]{1,0:T(8,128)(2,1)} %fusion.13.refs_0_, bf16[352,2048]{1,0:T(8,128)(2,1)} %fusion.12.refs_1_), custom_call_target="tpu_custom_call" | custom-call | flops 35433480192 | bytes 60293120 | tf_op jit(solution)/shard_map/outer/pallas_call | solution.py:634
  719.6 29.4 %outer.3 = bf16[8,2,128,2048]{3,2,1,0:T(8,128)(2,1)} custom-call(s32[16]{0:T(128)} %reshape.840.shard_ref, bf16[6,352,2048]{2,1,0:T(8,128)(2,1)} %get-tuple-element.98.h_ref.d_ref, bf16[8,176,2048]{2,1,0:T(8,128)(2,1)} %e_ref.3, bf16[704,2048]{1,0:T(8,128)(2,1)} %s_ref.3, bf16[8,256,256]{2,1,0:T(8,128)(2,1)} %broadcast_select_fusion.1.refs_0_, ...), custom_call_target="tpu_custom_call" | custom-call | flops 17716740096 | bytes 34340864 | tf_op jit(solution)/shard_map/outer/pallas_call | solution.py:634
  765.0 40.0 %all-to-all-done = bf16[8,256,256]{2,1,0:T(8,128)(2,1)S(1)} async-done(((bf16[8,256,256]{2,1,0:T(8,128)(2,1)}), bf16[8,256,256]{2,1,0:T(8,128)(2,1)S(1)}, u32[]{:S(2)}, u32[]{:S(2)}) %all-to-all-start) | async-done | bytes 1048608 | tf_op jit(solution)/shard_map/all_to_all | solution.py:1080
  807.5 21.4 %attend_back.2 = (bf16[2,8,2,64,256]{4,3,2,1,0:T(8,128)(2,1)}, bf16[4,2,2,512,256]{4,3,2,1,0:T(8,128)(2,1)}) custom-call(s32[1]{0:T(128)} %bitcast.c_ref, bf16[2,8,2,64,256]{4,3,2,1,0:T(8,128)(2,1)} %bitcast.648, bf16[4,2,2,512,256]{4,3,2,1,0:T(8,128)(2,1)} %pad_maximum_fusion.1.k_ref.v_ref, bf16[4,2,2,512,256]{4,3,2,1,0:T(8,128)(2,1)} %pad_maximum_fusion.1.k_ref.v_ref, ...), custom_call_target="tpu_custom_call" | custom-call | flops 12079595520 | bytes 12582912 | tf_op jit(solution)/shard_map/attend_back/pallas_call | solution.py:259
  832.0 20.9 %attend_back.3 = (bf16[2,8,2,64,256]{4,3,2,1,0:T(8,128)(2,1)}, bf16[4,2,2,512,256]{4,3,2,1,0:T(8,128)(2,1)}) custom-call(s32[1]{0:T(128)} %bitcast.c_ref, bf16[2,8,2,64,256]{4,3,2,1,0:T(8,128)(2,1)} %bitcast.649, bf16[4,2,2,512,256]{4,3,2,1,0:T(8,128)(2,1)} %pad_maximum_fusion.k_ref.v_ref, ...), custom_call_target="tpu_custom_call", output_to_operand_aliasing={{0}: (11, {})} | custom-call | flops 12079595520 | bytes 12582912 | tf_op jit(solution)/shard_map/attend_back/pallas_call | solution.py:259
  872.5 16.1 %collective-permute-done.66 = bf16[2,2,512,256]{3,2,1,0:T(8,128)(2,1)S(1)} collective-permute-done((bf16[2,2,512,256]{3,2,1,0:T(8,128)(2,1)S(1)}, bf16[2,2,512,256]{3,2,1,0:T(8,128)(2,1)S(1)}, u32[]{:S(2)}, u32[]{:S(2)}) %collective-permute-start.66) | collective-permute-done | bytes 1048608 | tf_op jit(solution)/shard_map/ppermute | solution.py:798
  891.7 19.4 %collective-permute-done.69 = bf16[2,2,512,256]{3,2,1,0:T(8,128)(2,1)S(1)} collective-permute-done((bf16[2,2,512,256]{3,2,1,0:T(8,128)(2,1)S(1)}, bf16[2,2,512,256]{3,2,1,0:T(8,128)(2,1)S(1)}, u32[]{:S(2)}, u32[]{:S(2)}) %collective-permute-start.69) | collective-permute-done | bytes 1048608 | tf_op jit(solution)/shard_map/ppermute | solution.py:798
  923.3 18.7 %collective-permute-done.64 = bf16[352,2048]{1,0:T(8,128)(2,1)} collective-permute-done((bf16[352,2048]{1,0:T(8,128)(2,1)S(1)}, bf16[352,2048]{1,0:T(8,128)(2,1)}, u32[]{:S(2)}, u32[]{:S(2)}) %collective-permute-start.64) | collective-permute-done | bytes 1441824 | tf_op jit(solution)/shard_map/ppermute | solution.py:815
  944.5 14.4 %project_back.1 = (bf16[3,2048,256]{2,1,0:T(8,128)(2,1)}, bf16[2048,2048]{1,0:T(8,128)(2,1)}, f32[8,2048]{1,0:T(8,128)S(1)}) custom-call(bf16[2048,256]{1,0:T(8,128)(2,1)S(1)} %bitcast.650, bf16[2,2,8,64,256]{4,3,2,1,0:T(8,128)(2,1)S(1)} %bitcast.641, bf16[2,2,8,64,256]{4,3,2,1,0:T(8,128)(2,1)S(1)} %bitcast.642, f32[2048,128]{1,0:T(8,128)S(1)} %bitcast.638, ...), custom_call_target="tpu_custom_call" | custom-call | flops 6442450944 | bytes 25165824 | tf_op jit(solution)/shard_map/project_back/pallas_call | solution.py:432
  963.9 11.5 fusion.1
  1064.3 17.1 %finish.6 = f32[2,4,352,2048]{3,2,1,0:T(8,128)} custom-call(s32[1]{0:T(128)} %bitcast.62.core_ref, bf16[352,2048]{1,0:T(8,128)(2,1)S(1)} %add_convert_fusion.6.refs_0_, bf16[352,2048]{1,0:T(8,128)(2,1)} %add_convert_fusion.5.refs_1_, bf16[352,2048]{1,0:T(8,128)(2,1)} %add_convert_fusion.4.refs_2_, bf16[352,2048]{1,0:T(8,128)(2,1)} %add_convert_fusion.3.refs_3_, ...), custom_call_target="tpu_custom_call" | custom-call | bytes 34603008 | tf_op jit(solution)/shard_map/finish/pallas_call | solution.py:728
  1099.8 27.5 %reduce-scatter.11.cloned.1.call-done = bf16[1,64,2048]{2,1,0:T(8,128)(2,1)} async-done(((bf16[8,64,2048]{2,1,0:T(8,128)(2,1)}), bf16[1,64,2048]{2,1,0:T(8,128)(2,1)}) %reduce-scatter.11.cloned.1.call-update) | async-done | bytes 262160 | tf_op jit(solution)/shard_map/reduce_scatter | solution.py:1133
  (724 shorter events, 579.2 us)
Async XLA Ops:
  7.2 203.6 %all-gather.5.cloned.1.call-start = ((), (), s32[]{:S(2)}) async-start(), calls=%async_computation.9 | async-start | bytes 2359296 | tf_op jit(solution)/shard_map/all_gather | solution.py:915
  15.3 407.3 %all-gather.7.cloned.1.call-start = ((), (), s32[]{:S(2)}) async-start(), calls=%async_computation.10 | async-start | bytes 9437184 | tf_op jit(solution)/shard_map/all_gather | solution.py:918
  168.2 416.0 %reduce-scatter.5.cloned.1.call-start = ((), (), s32[]{:S(2)}) async-start(), calls=%async_computation.5 | async-start | bytes 147456 | tf_op jit(solution)/shard_map/reduce_scatter | solution.py:982
  210.8 48.4 %collective-permute-start.35 = (bf16[8,64,2048]{2,1,0:T(8,128)(2,1)}, bf16[8,64,2048]{2,1,0:T(8,128)(2,1)}, u32[]{:S(2)}, u32[]{:S(2)}) collective-permute-start(bf16[8,64,2048]{2,1,0:T(8,128)(2,1)} %bitcast.32.refs_16_), channel_id=1, source_target_pairs={{0,16},{8,24},{16,0},{24,8},{1,17},{9,25},{17,1},{25,9},{2,18},{10... | collective-permute-start | bytes 6291464 | tf_op jit(solution)/shard_map/ppermute | solution.py:785
  255.8 119.6 %collective-permute-start.34 = (bf16[8,64,2048]{2,1,0:T(8,128)(2,1)}, bf16[8,64,2048]{2,1,0:T(8,128)(2,1)}, u32[]{:S(2)}, u32[]{:S(2)}) collective-permute-start(bf16[8,64,2048]{2,1,0:T(8,128)(2,1)} %bitcast.32.refs_16_), channel_id=1, source_target_pairs={{0,8},{8,0},{16,24},{24,16},{1,9},{9,1},{17,25},{25,17},{2,10},{10... | collective-permute-start | bytes 6291464 | tf_op jit(solution)/shard_map/ppermute | solution.py:787
  259.2 116.2 %collective-permute-start.36 = (bf16[8,64,2048]{2,1,0:T(8,128)(2,1)}, bf16[8,64,2048]{2,1,0:T(8,128)(2,1)}, u32[]{:S(2)}, u32[]{:S(2)}) collective-permute-start(bf16[8,64,2048]{2,1,0:T(8,128)(2,1)} %collective-permute-done.35.refs_18_), channel_id=1, source_target_pairs={{0,8},{8,0},{16,24},{24,16},{1,9},{9,1},{17,25},{25,17},{2,10},{10... | collective-permute-start | bytes 6291464 | tf_op jit(solution)/shard_map/ppermute | solution.py:787
  524.1 418.0 %reduce-scatter.7.cloned.1.call-start = ((), (), s32[]{:S(2)}) async-start(), calls=%async_computation.6 | async-start | bytes 9437184 | tf_op jit(solution)/shard_map/reduce_scatter | solution.py:1091
  586.4 46.9 %collective-permute-start.45 = (bf16[352,2048]{1,0:T(8,128)(2,1)}, bf16[352,2048]{1,0:T(8,128)(2,1)}, u32[]{:S(2)}, u32[]{:S(2)}) collective-permute-start(bf16[352,2048]{1,0:T(8,128)(2,1)} %fusion.13.refs_0_), channel_id=1, source_target_pairs={{0,16},{8,24},{16,0},{24,8},{1,17},{9,25},{17,1},{25,9},{2,18},{10... | collective-permute-start | bytes 4325384 | tf_op jit(solution)/shard_map/ppermute | solution.py:815
  587.8 74.1 %collective-permute-start.52 = (bf16[352,2048]{1,0:T(8,128)(2,1)}, bf16[352,2048]{1,0:T(8,128)(2,1)}, u32[]{:S(2)}, u32[]{:S(2)}) collective-permute-start(bf16[352,2048]{1,0:T(8,128)(2,1)} %fusion.12.refs_1_), channel_id=1, source_target_pairs={{0,16},{8,24},{16,0},{24,8},{1,17},{9,25},{17,1},{25,9},{2,18},{10... | collective-permute-start | bytes 4325384 | tf_op jit(solution)/shard_map/ppermute | solution.py:815
  644.8 61.7 %collective-permute-start.59 = (bf16[352,2048]{1,0:T(8,128)(2,1)}, bf16[352,2048]{1,0:T(8,128)(2,1)}, u32[]{:S(2)}, u32[]{:S(2)}) collective-permute-start(bf16[352,2048]{1,0:T(8,128)(2,1)} %fusion.11), channel_id=1, source_target_pairs={{0,16},{8,24},{16,0},{24,8},{1,17},{9,25},{17,1},{25,9},{2,18},{10... | collective-permute-start | bytes 4325384 | tf_op jit(solution)/shard_map/ppermute | solution.py:815
  664.2 55.4 %collective-permute-start.61 = (bf16[352,2048]{1,0:T(8,128)(2,1)}, bf16[352,2048]{1,0:T(8,128)(2,1)}, u32[]{:S(2)}, u32[]{:S(2)}) collective-permute-start(bf16[352,2048]{1,0:T(8,128)(2,1)} %fusion.10), channel_id=1, source_target_pairs={{0,16},{8,24},{16,0},{24,8},{1,17},{9,25},{17,1},{25,9},{2,18},{10... | collective-permute-start | bytes 4325384 | tf_op jit(solution)/shard_map/ppermute | solution.py:815
  749.1 55.9 %all-to-all-start = ((bf16[8,256,256]{2,1,0:T(8,128)(2,1)}), bf16[8,256,256]{2,1,0:T(8,128)(2,1)S(1)}, u32[]{:S(2)}, u32[]{:S(2)}) async-start(bf16[8,256,256]{2,1,0:T(8,128)(2,1)} %broadcast_select_fusion.1.refs_0_), calls=%async_computation.2 | async-start | bytes 2097152 | tf_op jit(solution)/shard_map/all_to_all | solution.py:1080
  752.6 336.2 %reduce-scatter.9.cloned.1.call-start = ((), (), s32[]{:S(2)}) async-start(), calls=%async_computation.7 | async-start | bytes 147456 | tf_op jit(solution)/shard_map/reduce_scatter | solution.py:1141
  752.8 54.8 %collective-permute-start.62 = (bf16[352,2048]{1,0:T(8,128)(2,1)}, bf16[352,2048]{1,0:T(8,128)(2,1)}, u32[]{:S(2)}, u32[]{:S(2)}) collective-permute-start(bf16[352,2048]{1,0:T(8,128)(2,1)} %fusion.9), channel_id=1, source_target_pairs={{0,16},{8,24},{16,0},{24,8},{1,17},{9,25},{17,1},{25,9},{2,18},{10... | collective-permute-start | bytes 4325384 | tf_op jit(solution)/shard_map/ppermute | solution.py:815
  754.2 77.8 %collective-permute-start.63 = (bf16[352,2048]{1,0:T(8,128)(2,1)}, bf16[352,2048]{1,0:T(8,128)(2,1)}, u32[]{:S(2)}, u32[]{:S(2)}) collective-permute-start(bf16[352,2048]{1,0:T(8,128)(2,1)} %fusion.8), channel_id=1, source_target_pairs={{0,16},{8,24},{16,0},{24,8},{1,17},{9,25},{17,1},{25,9},{2,18},{10... | collective-permute-start | bytes 4325384 | tf_op jit(solution)/shard_map/ppermute | solution.py:815
  757.5 108.2 %collective-permute-start.75 = (bf16[352,2048]{1,0:T(8,128)(2,1)}, bf16[352,2048]{1,0:T(8,128)(2,1)}, u32[]{:S(2)}, u32[]{:S(2)}) collective-permute-start(bf16[352,2048]{1,0:T(8,128)(2,1)} %slice_bitcast_fusion.2), channel_id=1, source_target_pairs={{0,8},{8,0},{16,24},{24,16},{1,9},{9,1},{17,25},{25,17},{2,10},{10... | collective-permute-start | bytes 4325384 | tf_op jit(solution)/shard_map/ppermute | solution.py:810
  764.4 149.3 %collective-permute-start.79 = (bf16[8,2,64,2048]{3,2,1,0:T(8,128)(2,1)}, bf16[8,2,64,2048]{3,2,1,0:T(8,128)(2,1)}, u32[]{:S(2)}, u32[]{:S(2)}) collective-permute-start(bf16[8,2,64,2048]{3,2,1,0:T(8,128)(2,1)} %dynamic-slice_bitcast_fusion), channel_id=1, source_target_pairs={{0,8},{8,0},{16,24},{24,16},{1,9},{9,1},{17,25},{25,17},{2,10},{10... | collective-permute-start | bytes 12582920 | tf_op jit(solution)/shard_map/ppermute | solution.py:1121
  871.3 70.8 %collective-permute-start.64 = (bf16[352,2048]{1,0:T(8,128)(2,1)S(1)}, bf16[352,2048]{1,0:T(8,128)(2,1)}, u32[]{:S(2)}, u32[]{:S(2)}) collective-permute-start(bf16[352,2048]{1,0:T(8,128)(2,1)S(1)} %copy-done.46), channel_id=1, source_target_pairs={{0,16},{8,24},{16,0},{24,8},{1,17},{9,25},{17,1},{25,9},{2,18},{10... | collective-permute-start | bytes 4325384 | tf_op jit(solution)/shard_map/ppermute | solution.py:815
  888.6 119.2 %collective-permute-start.76 = (bf16[352,2048]{1,0:T(8,128)(2,1)}, bf16[352,2048]{1,0:T(8,128)(2,1)}, u32[]{:S(2)}, u32[]{:S(2)}) collective-permute-start(bf16[352,2048]{1,0:T(8,128)(2,1)} %fusion.6), channel_id=1, source_target_pairs={{0,16},{8,24},{16,0},{24,8},{1,17},{9,25},{17,1},{25,9},{2,18},{10... | collective-permute-start | bytes 4325384 | tf_op jit(solution)/shard_map/ppermute | solution.py:815
  922.0 95.0 %collective-permute-start.80 = (bf16[8,64,2048]{2,1,0:T(8,128)(2,1)}, bf16[8,64,2048]{2,1,0:T(8,128)(2,1)}, u32[]{:S(2)}, u32[]{:S(2)}) collective-permute-start(bf16[8,64,2048]{2,1,0:T(8,128)(2,1)} %dynamic-slice_bitcast_fusion.1), channel_id=1, source_target_pairs={{0,16},{8,24},{16,0},{24,8},{1,17},{9,25},{17,1},{25,9},{2,18},{10... | collective-permute-start | bytes 6291464 | tf_op jit(solution)/shard_map/ppermute | solution.py:1123
  963.9 163.4 %reduce-scatter.11.cloned.1.call-start = ((), (), s32[]{:S(2)}) async-start(), calls=%async_computation.8 | async-start | bytes 2359296 | tf_op jit(solution)/shard_map/reduce_scatter | solution.py:1133
  1084.3 52.8 %collective-permute-start.94 = (bf16[1024,3,256]{2,0,1:T(8,128)(2,1)}, bf16[1024,3,256]{2,0,1:T(8,128)(2,1)}, u32[]{:S(2)}, u32[]{:S(2)}) collective-permute-start(bf16[1024,3,256]{2,0,1:T(8,128)(2,1)} %fusion.4), channel_id=1, source_target_pairs={{0,16},{8,24},{16,0},{24,8},{1,17},{9,25},{17,1},{25,9},{2,18},{10... | collective-permute-start | bytes 4718600 | tf_op jit(solution)/shard_map/ppermute | solution.py:815
  1088.8 47.8 %collective-permute-start.91 = (f32[16,256]{1,0:T(8,128)}, f32[16,256]{1,0:T(8,128)S(1)}, u32[]{:S(2)}, u32[]{:S(2)}) collective-permute-start(f32[16,256]{1,0:T(8,128)} %bitcast.717), channel_id=1, source_target_pairs={{0,8},{8,0},{16,24},{24,16},{1,9},{9,1},{17,25},{25,17},{2,10},{10... | collective-permute-start | bytes 49160 | tf_op jit(solution)/shard_map/ppermute | solution.py:1167
  1092.0 57.9 %collective-permute-start.98 = (bf16[352,2048]{1,0:T(8,128)(2,1)}, bf16[352,2048]{1,0:T(8,128)(2,1)}, u32[]{:S(2)}, u32[]{:S(2)}) collective-permute-start(bf16[352,2048]{1,0:T(8,128)(2,1)} %add_convert_fusion.9.refs_0_), channel_id=1, source_target_pairs={{0,8},{8,0},{16,24},{24,16},{1,9},{9,1},{17,25},{25,17},{2,10},{10... | collective-permute-start | bytes 4325384 | tf_op jit(solution)/shard_map/ppermute | solution.py:821
  (174 other events, 3046.3 us)
Sparse Core Ops, SparseCore 0:
  15.4 62.5 all-gather.4
  168.3 132.4 all-gather.6
  524.2 59.9 reduce-scatter.4
  749.2 168.8 reduce-scatter.6
  964.0 59.7 reduce-scatter.8
  1063.0 64.2 reduce-scatter.10

commit v2 on v1

--- a/solution.py
+++ b/solution.py
@@ -655,14 +655,22 @@
 
 
 def weight_kernel(blocks, core_ref, shard_ref, h_ref, *refs):
-    o_ref = refs[-1]
-    for lo in range(0, o_ref.shape[2], 512):
-        cols = slice(lo, lo + 512)
-        if blocks:
-            other = jnp.concatenate([ref[0, 0, :, cols] for ref in refs[:blocks]])
-        else:
-            other = refs[0][:, cols]
-        o_ref[0, :, cols] = dot(h_ref[0], other, 1, 0).astype(BF)
+    def run(o_ref):
+        for lo in range(0, o_ref.shape[1], 512):
+            cols = slice(lo, lo + 512)
+            if blocks:
+                other = jnp.concatenate([ref[0, 0, :, cols] for ref in refs[:blocks]])
+            else:
+                other = refs[0][:, cols]
+            o_ref[:, cols] = dot(h_ref[0], other, 1, 0).astype(BF)
+
+    @pl.when(pl.program_id(0) == core_ref[0])
+    def _():
+        run(refs[-2])
+
+    @pl.when(pl.program_id(0) != core_ref[0])
+    def _():
+        run(refs[-1])
 
 
 def weight_grad(core, shards, hid, other, base, stride, piece, pieces, *deps):
@@ -685,11 +693,9 @@
             ]
             + specs
             + [pl.BlockSpec(memory_space=pl.ANY)] * len(deps),
-            out_specs=pl.BlockSpec(
-                (1, units, width), lambda i, c, p: (lax.rem(i + c[0], 2), 0, 0)
-            ),
-        ),
-        out_shape=jax.ShapeDtypeStruct((2, units, width), BF),
+            out_specs=[pl.BlockSpec((units, width), lambda i, c, p: (0, 0))] * 2,
+        ),
+        out_shape=[jax.ShapeDtypeStruct((units, width), BF)] * 2,
         compiler_params=pltpu.CompilerParams(vmem_limit_bytes=40 * MIB),
         cost_estimate=pl.CostEstimate(
             flops=4 * units * tokens * width,
@@ -753,16 +759,21 @@
         pairs = [(self.order[i], self.order[(i + by) % n]) for i in range(n)]
         return lax.ppermute(value, "fsdp", pairs)
 
-    def gather(self, ahead, behind):
+    def gather(self, ahead, behind, first=()):
         a, b = [ahead], [behind]
-        for _ in range(self.count - 1):
-            a.append(self.shift(a[-1], 1))
-            b.append(self.shift(b[-1], -1))
+        for k in range(self.count - 1):
+            to_a, to_b = a[-1], b[-1]
+            if k == 1 and first:
+                to_a, to_b = after(to_a, *first), after(to_b, *first)
+            a.append(self.shift(to_a, 1))
+            b.append(self.shift(to_b, -1))
         return a, b
 
-    def scatter(self, ahead, behind, work=()):
+    def scatter(self, ahead, behind, work=(), first=()):
         n = self.count
         a, b = ahead(1), behind(1)
+        if first:
+            a, b = after(a, *first), after(b, *first)
         held = []
         for k in range(2, n + 1):
             kind = BF if k < n else F32
@@ -779,10 +790,13 @@
     return [(x * 2 + k, ((x + lanes) % half) * 2 + (k ^ core)) for x in range(half) for k in range(2)]
 
 
-def ctx_gather(value, ctx_count):
+def ctx_gather(value, ctx_count, *ties):
     got = []
     for lanes in range(ctx_count // 2):
-        mine = value if lanes == 0 else lax.ppermute(value, "ctx", ctx_pairs(ctx_count, lanes, 0))
+        mine = value
+        if lanes:
+            sent = after(value, *ties) if ties else value
+            mine = lax.ppermute(sent, "ctx", ctx_pairs(ctx_count, lanes, 0))
         got.append(mine)
         got.append(lax.ppermute(mine, "ctx", ctx_pairs(ctx_count, 0, 1)))
     return got
@@ -912,10 +926,9 @@
 
     share = local // ctx_count
     mine = lax.dynamic_slice_in_dim(attention_output_weights, c * share, share, 0)
-    out_piece = lax.all_gather(mine, "fsdp", axis=0)
-    out_pieces = ctx_gather(out_piece, ctx_count)
+    out_piece = lax.all_gather(after(mine, got_a[n - 2], got_b[n - 2]), "fsdp", axis=0)
     cot = jnp.transpose(cotangent[:, :, 0], (1, 0, 2, 3)).reshape(2, cut, width)
-    cot_all = lax.all_gather(after(cot, got_a[n - 3]), "fsdp", axis=0)
+    cot_all = lax.all_gather(after(cot, *last), "fsdp", axis=0)
     routes_in, priority_in = after(routes, got_a[5]), after(priority, got_a[5])
     kept_own = kept_table(
         routes_in.reshape(own_rows, top), priority_in.reshape(own_rows), experts, capacity
@@ -927,17 +940,23 @@
         all_rows, gain_one, attention_input_weights, flat_cos, flat_sin, seqs, n
     )
     query = query.reshape(2, n, seqs, pr, local)
+    pieces = [ctx_gather(kv_own[0], ctx_count)]
+    for s in range(1, seqs):
+        pieces.append(ctx_gather(kv_own[s], ctx_count, pieces[-1][2]))
     kvs = []
-    for s in range(seqs):
-        pieces = ctx_gather(kv_own[s], ctx_count)
-        kvs.append(jnp.stack(pieces).reshape(ctx_count, 2, 2, span, local))
-
     mixed, log_sums = None, []
     for s in range(seqs):
+        if s:
+            pieces[s] = [after(piece, mixed) for piece in pieces[s]]
+        kvs.append(jnp.stack(pieces[s]).reshape(ctx_count, 2, 2, span, local))
         mixed, lse = attend(c_arr, query, kvs[s], s, flag_col, flag_row, mixed)
         log_sums.append(lse)
     sent = mixed.reshape(2, tokens // 2, local)
-    got_a, got_b = ring.gather(jnp.concatenate([sent[0], kept_rows]), sent[1])
+    sent_after = mixed
+    got_a, got_b = ring.gather(
+        jnp.concatenate([sent[0], kept_rows]), sent[1], [cot_all]
+    )
+    out_pieces = ctx_gather(after(out_piece, sent_after), ctx_count)
     kept = [
         g[tokens // 2 :].reshape(-1)[: kept_own.size].reshape(experts, seqs, 2, pr) for g in got_a
     ]
@@ -1006,10 +1025,11 @@
                 *ties,
             )
         )
-        return sums[key].value
+        return sums[key].value[0]
 
     late = [("out", base, 0) for base, _ in spots]
     queue = [("in", base, piece) for base, _ in spots for piece in (0, 1)]
+    beside_in, after_in = queue[:-1], queue[-1:]
     flown = []
 
     def fly(key):
@@ -1029,25 +1049,27 @@
 
     def beside(k, a, b):
         held = []
-        if k - 2 < len(queue):
-            held.append(weight_piece(queue[k - 2], a, b))
-        if four and 0 <= k - 3 < len(queue):
-            held.append(sums[queue[k - 3]].reduce())
-            flown.append(sums[queue[k - 3]].cross(*flown[-2:-1]))
-        if k in (3, 5):
-            held += early_got[(k - 3) // 2]
+        if k - 2 < len(beside_in):
+            held.append(weight_piece(beside_in[k - 2], a, b))
+        if four and 0 <= k - 3 < len(beside_in):
+            held.append(sums[beside_in[k - 3]].reduce())
+            flown.append(sums[beside_in[k - 3]].cross(*flown[-2:-1]))
+        if k == 3:
+            held += early_got[1]
         if k == n - 1 and four:
-            held.append(sums[queue[0]].got)
+            held.append(sums[beside_in[0]].got)
         return held
 
-    gi_a, gi_b, _ = ring.scatter(lambda k: grad_in[k, 0], lambda k: grad_in[k, 1], beside)
-    for key in queue[n - 1 :]:
+    gi_a, gi_b, _ = ring.scatter(
+        lambda k: grad_in[k, 0], lambda k: grad_in[k, 1], beside, early_got[0]
+    )
+    for key in beside_in[n - 1 :]:
         weight_piece(key, gi_a, gi_b)
     if four:
-        for key in queue[n - 2 :]:
+        for key in beside_in[n - 2 :]:
             sums[key].reduce()
             flown.append(sums[key].cross(*flown[-2:-1]))
-    got_in = [sums[key].got for key in queue] if four else []
+    got_in = [sums[key].got for key in beside_in] if four else []
 
     def norm_back(grad, value, gain):
         inverse = lax.rsqrt(jnp.mean(value * value, axis=-1, keepdims=True) + EPSILON)
@@ -1090,7 +1112,21 @@
     ).reshape(hidden_in.shape)
     out_own = lax.psum_scatter(out_part, "fsdp", scatter_dimension=0, tiled=True)
 
+    lo = range(quarter)
+    hi = range(experts // 2, experts // 2 + halves)
+    done = {}
+
+    def finished(keys, gated, *ties):
+        for key in keys:
+            if key not in done:
+                done[key] = sums[key].finish(*ties)
+        kept_halves, got_halves = zip(*[done[key] for key in keys])
+        return finish(core_arr, kept_halves, got_halves, gated)
+
     d_q, pairs = None, []
+    if four:
+        for key in beside_in[:2]:
+            done[key] = sums[key].finish(out_part)
     for s in range(seqs):
         d_q, pair = attend_back(
             c_arr,
@@ -1105,12 +1141,12 @@
             flag_col,
             flag_row,
             d_q,
-            *got_in[2 + s : 3 + s],
+            *got_in[1 + s : 2 + s],
         )
+        if s and four:
+            pair = after(pair, *got_in[3:])
         pair = ctx_scatter([pair[j] for j in range(ctx_count)], ctx_count)
         pairs.append(pair.astype(BF).reshape(2, 2, n, pr, local))
-    d_q = after(d_q, out_own, *got_in[4:5])
-
     grad_out_own = dot(mixed_own.reshape(own_rows, width), branch, 0, 0).astype(BF)
     if four:
         flip, cross = ctx_pairs(4, 0, 1), ctx_pairs(4, 1, 0)
@@ -1123,36 +1159,43 @@
         quart_got = lax.ppermute(after(pick(part, 1 - lane, 1), *pairs), "ctx", cross)
     else:
         quart_got = lax.psum(grad_out_own, "ctx").reshape(n, local, width)
+    for key in after_in + late[2:]:
+        weight_piece(key, d_q)
+        if four:
+            sums[key].reduce()
+            sums[key].cross(*pairs)
+    if four:
+        total_expert_in = finished([("in", j, p) for j in lo for p in (0, 1)], False, d_q)
+        d_q = after(d_q, total_expert_in)
 
     raw, grad_n1, gain_part = project_back(
         d_q.reshape(tokens, local), pairs, flat_cos, flat_sin, attention_input_weights, all_rows
     )
-    quart_got = after(quart_got, raw)
-    quart = (pick(part, lane, 1).astype(F32) + quart_got.astype(F32)).astype(BF) if four else quart_got
-    quart = jnp.take(quart, by_shard, axis=0)
-    own_quart = lax.psum_scatter(quart, "fsdp", scatter_dimension=0, tiled=True)[0]
-
     grad_n1 = split(grad_n1)
     grad_gain_one = jnp.sum(gain_part, axis=0, keepdims=True)
     smalls_back = jnp.concatenate(
         [grad_gain_one, grad_gain_two, grad_small, jnp.zeros((16 - small_count, width), F32)]
     )
     smalls_back = jnp.transpose(smalls_back.reshape(16, n, slices), (1, 0, 2))
-    small_own = lax.psum_scatter(smalls_back, "fsdp", scatter_dimension=0, tiled=True)[0]
+    smalls_back = smalls_back.reshape(n, -1, width).astype(BF)
+    small_rows = smalls_back.shape[1]
+    smalls_back = jnp.pad(smalls_back, ((0, 0), (0, 8 - small_rows), (0, 0)))
+
+    ended = {}
 
     def beside_last(k, a, b):
         held = []
-        if k == 2:
-            held += [weight_piece(key, a, b) for key in late[2:]]
-        if k == 3 and four:
-            held += got_in[5:6]
-            for key in late[2:]:
-                sums[key].reduce()
-                sums[key].cross(quart_got)
-        if k == 5 and four:
-            held.append(quart_got)
+        if k == 3:
+            held.append(out_own)
+        if k == 3:
+            quart = after(quart_got, a)
+            if four:
+                quart = (pick(part, lane, 1).astype(F32) + quart.astype(F32)).astype(BF)
+            quart = jnp.take(quart, by_shard, axis=0)
+            quart = jnp.concatenate([quart, smalls_back], axis=1)
+            ended["out"] = lax.psum_scatter(quart, "fsdp", scatter_dimension=0, tiled=True)[0]
         if k == n - 1 and four:
-            held += [sums[key].got for key in late[2:]]
+            held += [sums[key].got for key in after_in]
         return held
 
     gn_a, gn_b, _ = ring.scatter(lambda k: grad_n1[0, k], lambda k: grad_n1[1, k], beside_last)
@@ -1162,7 +1205,9 @@
     grad_hidden = in_place((grad_mid + back_one).astype(BF))
     out_own = after(out_own, gn_a, gn_b).reshape(own_rows, width).astype(F32)
     layer_out = in_place((resid + out_own).astype(BF))
-    small_own = after(small_own, gn_a, gn_b)
+    own_quart = after(ended["out"], gn_a, gn_b)
+    small_own = own_quart[-8 : small_rows - 8].astype(F32).reshape(16, slices)
+    own_quart = own_quart[:-8]
     if ctx_count == 4:
         small_own = small_own + lax.ppermute(small_own, "ctx", ctx_pairs(4, 0, 1))
         small_own = small_own + lax.ppermute(small_own, "ctx", ctx_pairs(4, 1, 0))
@@ -1171,7 +1216,6 @@
 
     grad_attn_in = jnp.einsum("nd,jne->dje", normed_one, raw, preferred_element_type=F32)
 
-    own_quart = after(own_quart, gn_a, gn_b)
     if ctx_count == 4:
         t = own_quart
         o = lax.ppermute(t, "ctx", cross)
@@ -1183,17 +1227,7 @@
     else:
         total_attn_out = own_quart.astype(F32)
 
-    lo = range(quarter)
-    hi = range(experts // 2, experts // 2 + halves)
     if four:
-        done = {
-            key: value.finish(*([raw] if key in queue[:4] else [gn_a, gn_b]))
-            for key, value in sums.items()
-        }
-
-        def finished(keys, gated):
-            kept_halves, got_halves = zip(*[done[key] for key in keys])
-            return finish(core_arr, kept_halves, got_halves, gated)
 
         def halved(value):
             keep = lax.dynamic_index_in_dim(value, core, 0, keepdims=False)
@@ -1204,17 +1238,18 @@
             t, o = one.finish(gn_a, gn_b)
             return jnp.stack([jnp.where(core == 0, t, o), jnp.where(core == 0, o, t)]).astype(F32)
 
-        total_expert_in = finished([("in", j, p) for j in lo for p in (0, 1)], False)
-        total_expert_out = finished([("out", j, 0) for j in lo], False)
-        total_shared_in = finished([("in", j, p) for j in hi for p in (0, 1)], True)
-        total_shared_out = finished([("out", j, 0) for j in hi], False)
+        total_expert_out = finished([("out", j, 0) for j in lo], False, gn_a)
+        total_shared_in = finished([("in", j, p) for j in hi for p in (0, 1)], True, gn_a)
+        total_shared_out = finished([("out", j, 0) for j in hi], False, gn_a)
         total_attn_in = halved(grad_attn_in.reshape(2, width // 2, 3, local))
     else:
         first = core == 0
 
         def summed(keys, axis):
             values = [
-                jnp.where(first, sums[key].value, jnp.flip(sums[key].value, axis=0))
+                jnp.where(
+                    first, jnp.stack(sums[key].value), jnp.stack(sums[key].value[::-1])
+                )
                 for key in keys
             ]
             return lax.psum(jnp.stack(values, axis=axis), "ctx").astype(F32)

time: 1180 us -> 1160 us (0.983)
  waiting for transfers between devices: 412 us -> 360 us
  starting transfers between devices: 86.7 us -> 106 us
    ppermute x2, waiting for transfers between devices: 35.4 us -> 7.73 us  [ctx_scatter(): lax.ppermute(s.astype(BF), 'ctx', ctx_pairs(ctx_count, -lanes % half, 0))]
    ppermute x1, waiting for transfers between devices: 5.87 us -> 33 us  [per_device(): lax.ppermute(after(pick(part, 1 - lane, 1), *pairs), 'ctx', cross)]
    all_to_all x1, waiting for transfers between devices: 40 us -> 15.2 us  [per_device(): lax.all_to_all(grad_mixed, 'fsdp', split_axis=0, concat_axis=0, tiled=True)]
    ppermute x56, starting transfers between devices: 55.7 us -> 74.5 us  [shift(): return lax.ppermute(value, 'fsdp', pairs)]
    reduce_scatter x2 -> x1, waiting for transfers between devices: 27.5 us -> 11.8 us  [beside_last(): lax.psum_scatter(quart, 'fsdp', scatter_dimension=0, tiled=True)[0]]
    ppermute x56, waiting for transfers between devices: 243 us -> 227 us  [shift(): return lax.ppermute(value, 'fsdp', pairs)]
    squeeze x9 -> x0, local copies, waits for them, and re-layouts: 11.8 us -> none  [reduce(): keep, send = (self.value[0], self.value[1])]
    unnamed x234 -> x314, local copies, waits for them, and re-layouts: 38.4 us -> 48.4 us
  transfers between devices with their start and end apart: 114 -> 113, of which waited for: 47 -> 49; matrix products, arithmetic and copies ran while one was open for 20% -> 20% of each run, Pallas kernels for 24% -> 21%
where the time goes in v2:
time: 1160 us
  Pallas kernels  404 us (35%)
  waiting for transfers between devices  360 us (31%)
  other arithmetic  132 us (11%)
  local copies, waits for them, and re-layouts  112 us (10%)
  starting transfers between devices  106 us (9%)
  matrix products  24.6 us (2%)
  between operations  16.3 us (1%)
    ppermute x56, waiting for transfers between devices, shift(): return lax.ppermute(value, 'fsdp', pairs)  227 us
    pallas_call x9, Pallas kernels, weight_grad(): pl.pallas_call(functools.partial(weight_kernel, len(specs) if other.ndim...  80.3 us
    pallas_call x2, Pallas kernels, outer(): pl.pallas_call(functools.partial(outer_kernel, last + 1) if shards is not...  78.6 us
    ppermute x56, starting transfers between devices, shift(): return lax.ppermute(value, 'fsdp', pairs)  74.5 us
    pallas_call x1, Pallas kernels, inner(): pl.pallas_call(functools.partial(inner_kernel, expert_in.shape[0] // 2, 2...  72.9 us
    unnamed x314, local copies, waits for them, and re-layouts  48.4 us
    pallas_call x2, Pallas kernels, attend_back(): pl.pallas_call(functools.partial(attend_back_kernel, ctx_count), grid_spe...  42.4 us
    pallas_call x1, Pallas kernels, merge(): pl.pallas_call(functools.partial(merge_kernel, n, ctx_count), grid_spec=p...  39.5 us
  transfers between devices with their start and end apart: 113, of which 49 were waited for; matrix products, arithmetic and copies ran while one was open for 20% of the time, Pallas kernels for 21%

profile of v2, /device:TPU:0, one launch (start us, length us, event | category | flops | bytes accessed | tf_op | source)
XLA Modules:
  0.0 1155.2 jit_solution(2838107597856868089)
XLA Ops:
  14.5 12.6 %collective-permute-done = bf16[136,2048]{1,0:T(8,128)(2,1)S(1)} collective-permute-done((bf16[136,2048]{1,0:T(8,128)(2,1)S(1)}, bf16[136,2048]{1,0:T(8,128)(2,1)S(1)}, u32[]{:S(2)}, u32[]{:S(2)}) %collective-permute-start) | collective-permute-done | bytes 557088 | tf_op jit(solution)/shard_map/ppermute | solution.py:760
  29.1 11.8 %collective-permute-done.1 = bf16[136,2048]{1,0:T(8,128)(2,1)S(1)} collective-permute-done((bf16[136,2048]{1,0:T(8,128)(2,1)S(1)}, bf16[136,2048]{1,0:T(8,128)(2,1)S(1)}, u32[]{:S(2)}, u32[]{:S(2)}) %collective-permute-start.1) | collective-permute-done | bytes 557088 | tf_op jit(solution)/shard_map/ppermute | solution.py:760
  42.9 10.9 collective-permute-done.2
  68.6 10.5 collective-permute-done.4
  101.6 13.2 %collective-permute-done.13 = bf16[128,2048]{1,0:T(8,128)(2,1)} collective-permute-done((bf16[128,2048]{1,0:T(8,128)(2,1)}, bf16[128,2048]{1,0:T(8,128)(2,1)}, u32[]{:S(2)}, u32[]{:S(2)}) %collective-permute-start.13) | collective-permute-done | bytes 524320 | tf_op jit(solution)/shard_map/ppermute | solution.py:760
  139.5 13.2 %project.1 = (bf16[2048,2048]{1,0:T(8,128)(2,1)}, bf16[2048,256]{1,0:T(8,128)(2,1)S(1)}, bf16[2,2,2,8,64,256]{5,4,3,2,1,0:T(8,128)(2,1)S(1)}) custom-call(bf16[2048,2048]{1,0:T(8,128)(2,1)} %constant_dynamic-update-slice_fusion.h_ref.refs_20_.refs_5_, f32[1,2048]{1,0:T(1,128)S(1)} %bitcast.580, bf16[3,2048,256]{2,1,0:T(8,128)(2,1)S(1)} %copy-done.29, ...), custom_call_target="tpu_custom_call" | custom-call | flops 6442450944 | bytes 16777216 | tf_op jit(solution)/shard_map/project/pallas_call | solution.py:75
  155.6 23.3 %collective-permute-done.15 = bf16[2,2,8,64,256]{4,3,2,1,0:T(8,128)(2,1)} collective-permute-done((bf16[2,2,8,64,256]{4,3,2,1,0:T(8,128)(2,1)}, bf16[2,2,8,64,256]{4,3,2,1,0:T(8,128)(2,1)}, u32[]{:S(2)}, u32[]{:S(2)}) %collective-permute-start.15) | collective-permute-done | bytes 1048608 | tf_op jit(solution)/shard_map/ppermute | solution.py:799
  198.4 15.8 %attend.2 = (bf16[2,8,2,64,256]{4,3,2,1,0:T(8,128)(2,1)S(1)}, f32[2,2,8,512]{3,2,1,0:T(8,128)S(1)}) custom-call(s32[1]{0:T(128)} %bitcast.c_ref, bf16[2,8,2,64,256]{4,3,2,1,0:T(8,128)(2,1)S(1)} %bitcast.585, bf16[4,2,2,512,256]{4,3,2,1,0:T(8,128)(2,1)} %pad_maximum_fusion.k_ref.v_ref, bf16[4,2,2,512,256]{4,3,2,1,0:T(8,128)(2,1)} %pad_maximum_fusion.k_ref.v_ref, ...), custom_call_target="tpu_custom_call" | custom-call | flops 4831838208 | bytes 8388608 | tf_op jit(solution)/shard_map/attend/pallas_call | solution.py:161
  218.4 15.8 %attend.3 = (bf16[2,8,2,64,256]{4,3,2,1,0:T(8,128)(2,1)S(1)}, f32[2,2,8,512]{3,2,1,0:T(8,128)S(1)}) custom-call(s32[1]{0:T(128)} %bitcast.c_ref, bf16[2,8,2,64,256]{4,3,2,1,0:T(8,128)(2,1)S(1)} %bitcast.586, bf16[4,2,2,512,256]{4,3,2,1,0:T(8,128)(2,1)} %pad_maximum_fusion.1.k_ref.v_ref, ...), custom_call_target="tpu_custom_call", output_to_operand_aliasing={{0}: (6, {})} | custom-call | flops 4831838208 | bytes 8388608 | tf_op jit(solution)/shard_map/attend/pallas_call | solution.py:161
  239.3 16.4 %collective-permute-start.20 = (bf16[1032,256]{1,0:T(8,128)(2,1)S(1)}, bf16[1032,256]{1,0:T(8,128)(2,1)S(1)}, u32[]{:S(2)}, u32[]{:S(2)}) collective-permute-start(bf16[1032,256]{1,0:T(8,128)(2,1)S(1)} %pad_maximum_fusion.4.refs_0_), channel_id=1, source_target_pairs={{0,2},{2,4},{4,6},{6,7},{7,5},{5,3},{3,1},{1,0},{8,10},{10,12},{12... | collective-permute-start | bytes 1585160 | tf_op jit(solution)/shard_map/ppermute | solution.py:760
  257.7 18.5 %collective-permute-done.20.refs_1_ = bf16[1032,256]{1,0:T(8,128)(2,1)S(1)} collective-permute-done((bf16[1032,256]{1,0:T(8,128)(2,1)S(1)}, bf16[1032,256]{1,0:T(8,128)(2,1)S(1)}, u32[]{:S(2)}, u32[]{:S(2)}) %collective-permute-start.20) | collective-permute-done | bytes 528416 | tf_op jit(solution)/shard_map/ppermute | solution.py:760
  353.9 39.5 %merge.1 = (bf16[2048,2048]{1,0:T(8,128)(2,1)}, f32[2,128,2048]{2,1,0:T(8,128)}, f32[16,2048]{1,0:T(8,128)}, bf16[8,256,2048]{2,1,0:T(8,128)(2,1)}, bf16[2,128,2048]{2,1,0:T(8,128)(2,1)}) custom-call(s32[1]{0:T(128)} %bitcast.c_ref, s32[16]{0:T(128)} %reshape.833.shard_ref, bf16[1032,256]{1,0:T(8,128)(2,1)} %copy-done.71, bf16[1032,256]{1,0:T(8,128)(2,1)} %copy-done.113, ...), custom_call_target="tpu_custom_call" | custom-call | flops 17179869184 | bytes 33554432 | tf_op jit(solution)/shard_map/merge/pallas_call | solution.py:356
  399.6 72.9 %inner.1 = (bf16[6,704,2048]{2,1,0:T(8,128)(2,1)}, bf16[6,352,2048]{2,1,0:T(8,128)(2,1)}, f32[6,8,2048]{2,1,0:T(8,128)}) custom-call(s32[16]{0:T(128)} %reshape.833.shard_ref, bf16[2048,2048]{1,0:T(8,128)(2,1)} %get-tuple-element.130.x_ref.refs_0_, bf16[8,2,128,2048]{3,2,1,0:T(8,128)(2,1)} %bitcast.504, bf16[8,2,128,2048]{3,2,1,0:T(8,128)(2,1)} %bitcast.505, ...), custom_call_target="tpu_custom_call" | custom-call | flops 53150220288 | bytes 42729472 | tf_op jit(solution)/shard_map/inner/pallas_call | solution.py:553
  509.5 49.7 %outer.2 = bf16[8,2,128,2048]{3,2,1,0:T(8,128)(2,1)} custom-call(bf16[6,704,2048]{2,1,0:T(8,128)(2,1)} %get-tuple-element.133.d_ref.h_ref, bf16[8,2,176,2048]{3,2,1,0:T(8,128)(2,1)} %e_ref.2, bf16[2,704,2048]{2,1,0:T(8,128)(2,1)} %s_ref.2, bf16[352,2048]{1,0:T(8,128)(2,1)} %copy-done.44, bf16[352,2048]{1,0:T(8,128)(2,1)} %add_convert_fusion.17.refs_1_), custom_call_target="tpu_custom_call" | custom-call | flops 35433480192 | bytes 60293120 | tf_op jit(solution)/shard_map/outer/pallas_call | solution.py:634
  697.4 28.9 %outer.3 = bf16[8,2,128,2048]{3,2,1,0:T(8,128)(2,1)} custom-call(s32[16]{0:T(128)} %reshape.833.shard_ref, bf16[6,352,2048]{2,1,0:T(8,128)(2,1)} %get-tuple-element.132.h_ref.d_ref, bf16[8,176,2048]{2,1,0:T(8,128)(2,1)} %e_ref.3, bf16[704,2048]{1,0:T(8,128)(2,1)} %s_ref.3, bf16[8,256,256]{2,1,0:T(8,128)(2,1)} %broadcast_select_fusion.1.refs_0_, ...), custom_call_target="tpu_custom_call" | custom-call | flops 17716740096 | bytes 34340864 | tf_op jit(solution)/shard_map/outer/pallas_call | solution.py:634
  741.3 21.0 %collective-permute-done.62.refs_1_ = bf16[352,2048]{1,0:T(8,128)(2,1)} collective-permute-done((bf16[352,2048]{1,0:T(8,128)(2,1)S(1)}, bf16[352,2048]{1,0:T(8,128)(2,1)}, u32[]{:S(2)}, u32[]{:S(2)}) %collective-permute-start.62) | collective-permute-done | bytes 1441824 | tf_op jit(solution)/shard_map/ppermute | solution.py:829
  770.1 15.2 %all-to-all-done = bf16[8,256,256]{2,1,0:T(8,128)(2,1)S(1)} async-done(((bf16[8,256,256]{2,1,0:T(8,128)(2,1)}), bf16[8,256,256]{2,1,0:T(8,128)(2,1)S(1)}, u32[]{:S(2)}, u32[]{:S(2)}) %all-to-all-start) | async-done | bytes 1048608 | tf_op jit(solution)/shard_map/all_to_all | solution.py:1102
  790.1 21.0 %attend_back.2 = (bf16[2,8,2,64,256]{4,3,2,1,0:T(8,128)(2,1)}, bf16[4,2,2,512,256]{4,3,2,1,0:T(8,128)(2,1)}) custom-call(s32[1]{0:T(128)} %bitcast.c_ref, bf16[2,8,2,64,256]{4,3,2,1,0:T(8,128)(2,1)} %bitcast.583, bf16[4,2,2,512,256]{4,3,2,1,0:T(8,128)(2,1)} %pad_maximum_fusion.k_ref.v_ref, bf16[4,2,2,512,256]{4,3,2,1,0:T(8,128)(2,1)} %pad_maximum_fusion.k_ref.v_ref, ...), custom_call_target="tpu_custom_call" | custom-call | flops 12079595520 | bytes 12582912 | tf_op jit(solution)/shard_map/attend_back/pallas_call | solution.py:259
  811.2 21.4 %attend_back.3 = (bf16[2,8,2,64,256]{4,3,2,1,0:T(8,128)(2,1)}, bf16[4,2,2,512,256]{4,3,2,1,0:T(8,128)(2,1)}) custom-call(s32[1]{0:T(128)} %bitcast.c_ref, bf16[2,8,2,64,256]{4,3,2,1,0:T(8,128)(2,1)} %bitcast.584, bf16[4,2,2,512,256]{4,3,2,1,0:T(8,128)(2,1)} %pad_maximum_fusion.1.k_ref.v_ref, ...), custom_call_target="tpu_custom_call", output_to_operand_aliasing={{0}: (11, {})} | custom-call | flops 12079595520 | bytes 12582912 | tf_op jit(solution)/shard_map/attend_back/pallas_call | solution.py:259
  883.6 13.2 %finish.4 = f32[2,4,352,2048]{3,2,1,0:T(8,128)} custom-call(s32[1]{0:T(128)} %bitcast.62.core_ref, bf16[352,2048]{1,0:T(8,128)(2,1)} %add_convert_fusion.11.refs_0_, bf16[352,2048]{1,0:T(8,128)(2,1)S(1)} %add_convert_fusion.10.refs_1_, bf16[352,2048]{1,0:T(8,128)(2,1)S(1)} %copy-done.5, bf16[352,2048]{1,0:T(8,128)(2,1)S(1)} %add_convert_fusion.8.refs_3_, ...), custom_call_target="tpu_custom_call" | custom-call | bytes 34603008 | tf_op jit(solution)/shard_map/finish/pallas_call | solution.py:734
  909.8 14.6 %project_back.1 = (bf16[3,2048,256]{2,1,0:T(8,128)(2,1)}, bf16[2048,2048]{1,0:T(8,128)(2,1)}, f32[8,2048]{1,0:T(8,128)S(1)}) custom-call(bf16[2048,256]{1,0:T(8,128)(2,1)S(1)} %bitcast.573, bf16[2,2,8,64,256]{4,3,2,1,0:T(8,128)(2,1)S(1)} %bitcast.579, bf16[2,2,8,64,256]{4,3,2,1,0:T(8,128)(2,1)S(1)} %bitcast.578, f32[2048,128]{1,0:T(8,128)S(1)} %bitcast.575, ...), custom_call_target="tpu_custom_call" | custom-call | flops 6442450944 | bytes 25165824 | tf_op jit(solution)/shard_map/project_back/pallas_call | solution.py:432
  974.1 33.0 %collective-permute-done.92 = bf16[8,64,2048]{2,1,0:T(8,128)(2,1)S(1)} collective-permute-done((bf16[8,64,2048]{2,1,0:T(8,128)(2,1)}, bf16[8,64,2048]{2,1,0:T(8,128)(2,1)S(1)}, u32[]{:S(2)}, u32[]{:S(2)}) %collective-permute-start.92) | collective-permute-done | bytes 2097184 | tf_op jit(solution)/shard_map/ppermute | solution.py:1159
  1042.1 17.8 %collective-permute-done.80 = bf16[128,2048]{1,0:T(8,128)(2,1)S(1)} collective-permute-done((bf16[128,2048]{1,0:T(8,128)(2,1)S(1)}, bf16[128,2048]{1,0:T(8,128)(2,1)S(1)}, u32[]{:S(2)}, u32[]{:S(2)}) %collective-permute-start.80) | collective-permute-done | bytes 524320 | tf_op jit(solution)/shard_map/ppermute | solution.py:760
  1091.0 11.8 %reduce-scatter.8.cloned.1.call-done = bf16[1,72,2048]{2,1,0:T(8,128)(2,1)} async-done(((bf16[8,72,2048]{2,1,0:T(8,128)(2,1)}), bf16[1,72,2048]{2,1,0:T(8,128)(2,1)}) %reduce-scatter.8.cloned.1.call-update) | async-done | bytes 294928 | tf_op jit(solution)/shard_map/reduce_scatter | solution.py:1196
  (800 shorter events, 617.1 us)
Async XLA Ops:
  7.2 227.6 %all-gather.7.cloned.1.call-start = ((), (), s32[]{:S(2)}) async-start(), calls=%async_computation.8 | async-start | bytes 2359296 | tf_op jit(solution)/shard_map/all_gather | solution.py:929
  90.1 187.0 %all-gather.5.cloned.1.call-start = ((), (), s32[]{:S(2)}) async-start(), calls=%async_computation.7 | async-start | bytes 9437184 | tf_op jit(solution)/shard_map/all_gather | solution.py:931
  115.7 545.8 %reduce-scatter.4.cloned.1.call-start = ((), (), s32[]{:S(2)}) async-start(), calls=%async_computation.4 | async-start | bytes 147456 | tf_op jit(solution)/shard_map/reduce_scatter | solution.py:1001
  234.8 48.7 %collective-permute-start.35 = (bf16[8,64,2048]{2,1,0:T(8,128)(2,1)}, bf16[8,64,2048]{2,1,0:T(8,128)(2,1)}, u32[]{:S(2)}, u32[]{:S(2)}) collective-permute-start(bf16[8,64,2048]{2,1,0:T(8,128)(2,1)} %bitcast.36.refs_16_), channel_id=1, source_target_pairs={{0,16},{8,24},{16,0},{24,8},{1,17},{9,25},{17,1},{25,9},{2,18},{10... | collective-permute-start | bytes 6291464 | tf_op jit(solution)/shard_map/ppermute | solution.py:799
  257.7 88.7 %collective-permute-start.34 = (bf16[8,64,2048]{2,1,0:T(8,128)(2,1)}, bf16[8,64,2048]{2,1,0:T(8,128)(2,1)}, u32[]{:S(2)}, u32[]{:S(2)}) collective-permute-start(bf16[8,64,2048]{2,1,0:T(8,128)(2,1)} %bitcast.36.refs_16_), channel_id=1, source_target_pairs={{0,8},{8,0},{16,24},{24,16},{1,9},{9,1},{17,25},{25,17},{2,10},{10... | collective-permute-start | bytes 6291464 | tf_op jit(solution)/shard_map/ppermute | solution.py:801
  283.5 62.8 %collective-permute-start.36 = (bf16[8,64,2048]{2,1,0:T(8,128)(2,1)}, bf16[8,64,2048]{2,1,0:T(8,128)(2,1)}, u32[]{:S(2)}, u32[]{:S(2)}) collective-permute-start(bf16[8,64,2048]{2,1,0:T(8,128)(2,1)} %collective-permute-done.35.refs_18_), channel_id=1, source_target_pairs={{0,8},{8,0},{16,24},{24,16},{1,9},{9,1},{17,25},{25,17},{2,10},{10... | collective-permute-start | bytes 6291464 | tf_op jit(solution)/shard_map/ppermute | solution.py:801
  503.9 56.8 %collective-permute-start.39 = (bf16[352,2048]{1,0:T(8,128)(2,1)S(1)}, bf16[352,2048]{1,0:T(8,128)(2,1)}, u32[]{:S(2)}, u32[]{:S(2)}) collective-permute-start(bf16[352,2048]{1,0:T(8,128)(2,1)S(1)} %add_convert_fusion.18.refs_0_), channel_id=1, source_target_pairs={{0,16},{8,24},{16,0},{24,8},{1,17},{9,25},{17,1},{25,9},{2,18},{10... | collective-permute-start | bytes 4325384 | tf_op jit(solution)/shard_map/ppermute | solution.py:829
  563.4 443.6 %reduce-scatter.6.cloned.1.call-start = ((), (), s32[]{:S(2)}) async-start(), calls=%async_computation.5 | async-start | bytes 9437184 | tf_op jit(solution)/shard_map/reduce_scatter | solution.py:1113
  565.9 46.8 %collective-permute-start.46 = (bf16[352,2048]{1,0:T(8,128)(2,1)S(1)}, bf16[352,2048]{1,0:T(8,128)(2,1)S(1)}, u32[]{:S(2)}, u32[]{:S(2)}) collective-permute-start(bf16[352,2048]{1,0:T(8,128)(2,1)S(1)} %copy-done.46), channel_id=1, source_target_pairs={{0,16},{8,24},{16,0},{24,8},{1,17},{9,25},{17,1},{25,9},{2,18},{10... | collective-permute-start | bytes 4325384 | tf_op jit(solution)/shard_map/ppermute | solution.py:829
  611.9 67.6 %collective-permute-start.58 = (bf16[352,2048]{1,0:T(8,128)(2,1)}, bf16[352,2048]{1,0:T(8,128)(2,1)}, u32[]{:S(2)}, u32[]{:S(2)}) collective-permute-start(bf16[352,2048]{1,0:T(8,128)(2,1)} %add_convert_fusion.16), channel_id=1, source_target_pairs={{0,16},{8,24},{16,0},{24,8},{1,17},{9,25},{17,1},{25,9},{2,18},{10... | collective-permute-start | bytes 4325384 | tf_op jit(solution)/shard_map/ppermute | solution.py:829
  729.7 55.7 %all-to-all-start = ((bf16[8,256,256]{2,1,0:T(8,128)(2,1)}), bf16[8,256,256]{2,1,0:T(8,128)(2,1)S(1)}, u32[]{:S(2)}, u32[]{:S(2)}) async-start(bf16[8,256,256]{2,1,0:T(8,128)(2,1)} %broadcast_select_fusion.1.refs_0_), calls=%async_computation.2 | async-start | bytes 2097152 | tf_op jit(solution)/shard_map/all_to_all | solution.py:1102
  733.3 369.5 %reduce-scatter.8.cloned.1.call-start = ((), (), s32[]{:S(2)}) async-start(), calls=%async_computation.6 | async-start | bytes 2654208 | tf_op jit(solution)/shard_map/reduce_scatter | solution.py:1196
  740.7 91.9 %collective-permute-start.63 = (bf16[352,2048]{1,0:T(8,128)(2,1)}, bf16[352,2048]{1,0:T(8,128)(2,1)}, u32[]{:S(2)}, u32[]{:S(2)}) collective-permute-start(bf16[352,2048]{1,0:T(8,128)(2,1)} %add_convert_fusion.13), channel_id=1, source_target_pairs={{0,16},{8,24},{16,0},{24,8},{1,17},{9,25},{17,1},{25,9},{2,18},{10... | collective-permute-start | bytes 4325384 | tf_op jit(solution)/shard_map/ppermute | solution.py:829
  762.3 70.2 %collective-permute-start.71 = (bf16[352,2048]{1,0:T(8,128)(2,1)}, bf16[352,2048]{1,0:T(8,128)(2,1)}, u32[]{:S(2)}, u32[]{:S(2)}) collective-permute-start(bf16[352,2048]{1,0:T(8,128)(2,1)} %add_convert_fusion.12), channel_id=1, source_target_pairs={{0,16},{8,24},{16,0},{24,8},{1,17},{9,25},{17,1},{25,9},{2,18},{10... | collective-permute-start | bytes 4325384 | tf_op jit(solution)/shard_map/ppermute | solution.py:829
  766.0 91.7 %collective-permute-start.65 = (bf16[352,2048]{1,0:T(8,128)(2,1)S(1)}, bf16[352,2048]{1,0:T(8,128)(2,1)}, u32[]{:S(2)}, u32[]{:S(2)}) collective-permute-start(bf16[352,2048]{1,0:T(8,128)(2,1)S(1)} %add_convert_fusion.10.refs_1_), channel_id=1, source_target_pairs={{0,8},{8,0},{16,24},{24,16},{1,9},{9,1},{17,25},{25,17},{2,10},{10... | collective-permute-start | bytes 4325384 | tf_op jit(solution)/shard_map/ppermute | solution.py:835
  769.6 88.4 %collective-permute-start.64 = (bf16[352,2048]{1,0:T(8,128)(2,1)}, bf16[352,2048]{1,0:T(8,128)(2,1)}, u32[]{:S(2)}, u32[]{:S(2)}) collective-permute-start(bf16[352,2048]{1,0:T(8,128)(2,1)} %add_convert_fusion.11.refs_0_), channel_id=1, source_target_pairs={{0,8},{8,0},{16,24},{24,16},{1,9},{9,1},{17,25},{25,17},{2,10},{10... | collective-permute-start | bytes 4325384 | tf_op jit(solution)/shard_map/ppermute | solution.py:835
  854.7 88.3 %collective-permute-start.91 = (bf16[8,2,64,2048]{3,2,1,0:T(8,128)(2,1)}, bf16[8,2,64,2048]{3,2,1,0:T(8,128)(2,1)}, u32[]{:S(2)}, u32[]{:S(2)}) collective-permute-start(bf16[8,2,64,2048]{3,2,1,0:T(8,128)(2,1)} %dynamic-slice_bitcast_fusion), channel_id=1, source_target_pairs={{0,8},{8,0},{16,24},{24,16},{1,9},{9,1},{17,25},{25,17},{2,10},{10... | collective-permute-start | bytes 12582920 | tf_op jit(solution)/shard_map/ppermute | solution.py:1157
  861.5 45.8 %collective-permute-start.69 = (bf16[2,2,512,256]{3,2,1,0:T(8,128)(2,1)}, bf16[2,2,512,256]{3,2,1,0:T(8,128)(2,1)}, u32[]{:S(2)}, u32[]{:S(2)}) collective-permute-start(bf16[2,2,512,256]{3,2,1,0:T(8,128)(2,1)} %fusion.12), channel_id=1, source_target_pairs={{0,16},{8,24},{16,0},{24,8},{1,17},{9,25},{17,1},{25,9},{2,18},{10... | collective-permute-start | bytes 3145736 | tf_op jit(solution)/shard_map/ppermute | solution.py:812
  896.8 143.3 %collective-permute-start.82 = (bf16[352,2048]{1,0:T(8,128)(2,1)}, bf16[352,2048]{1,0:T(8,128)(2,1)}, u32[]{:S(2)}, u32[]{:S(2)}) collective-permute-start(bf16[352,2048]{1,0:T(8,128)(2,1)} %get-tuple-element.185), channel_id=1, source_target_pairs={{0,8},{8,0},{16,24},{24,16},{1,9},{9,1},{17,25},{25,17},{2,10},{10... | collective-permute-start | bytes 4325384 | tf_op jit(solution)/shard_map/ppermute | solution.py:824
  929.5 145.3 %collective-permute-start.97 = (bf16[352,2048]{1,0:T(8,128)(2,1)}, bf16[352,2048]{1,0:T(8,128)(2,1)}, u32[]{:S(2)}, u32[]{:S(2)}) collective-permute-start(bf16[352,2048]{1,0:T(8,128)(2,1)} %add_convert_fusion.6), channel_id=1, source_target_pairs={{0,16},{8,24},{16,0},{24,8},{1,17},{9,25},{17,1},{25,9},{2,18},{10... | collective-permute-start | bytes 4325384 | tf_op jit(solution)/shard_map/ppermute | solution.py:829
  949.8 57.2 %collective-permute-start.92 = (bf16[8,64,2048]{2,1,0:T(8,128)(2,1)}, bf16[8,64,2048]{2,1,0:T(8,128)(2,1)S(1)}, u32[]{:S(2)}, u32[]{:S(2)}) collective-permute-start(bf16[8,64,2048]{2,1,0:T(8,128)(2,1)} %dynamic-slice_bitcast_fusion.1), channel_id=1, source_target_pairs={{0,16},{8,24},{16,0},{24,8},{1,17},{9,25},{17,1},{25,9},{2,18},{10... | collective-permute-start | bytes 6291464 | tf_op jit(solution)/shard_map/ppermute | solution.py:1159
  971.5 100.3 %collective-permute-start.95 = (bf16[1024,3,256]{2,0,1:T(8,128)(2,1)}, bf16[1024,3,256]{2,0,1:T(8,128)(2,1)}, u32[]{:S(2)}, u32[]{:S(2)}) collective-permute-start(bf16[1024,3,256]{2,0,1:T(8,128)(2,1)} %fusion.29), channel_id=1, source_target_pairs={{0,8},{8,0},{16,24},{24,16},{1,9},{9,1},{17,25},{25,17},{2,10},{10... | collective-permute-start | bytes 4718600 | tf_op jit(solution)/shard_map/ppermute | solution.py:824
  1074.8 41.7 %collective-permute-start.98 = (bf16[1024,3,256]{2,0,1:T(8,128)(2,1)}, bf16[1024,3,256]{2,0,1:T(8,128)(2,1)}, u32[]{:S(2)}, u32[]{:S(2)}) collective-permute-start(bf16[1024,3,256]{2,0,1:T(8,128)(2,1)} %fusion.5), channel_id=1, source_target_pairs={{0,16},{8,24},{16,0},{24,8},{1,17},{9,25},{17,1},{25,9},{2,18},{10... | collective-permute-start | bytes 4718600 | tf_op jit(solution)/shard_map/ppermute | solution.py:829
  1079.6 51.9 %collective-permute-start.106 = (bf16[352,2048]{1,0:T(8,128)(2,1)S(1)}, bf16[352,2048]{1,0:T(8,128)(2,1)}, u32[]{:S(2)}, u32[]{:S(2)}) collective-permute-start(bf16[352,2048]{1,0:T(8,128)(2,1)S(1)} %add_convert_fusion.1.refs_1_), channel_id=1, source_target_pairs={{0,8},{8,0},{16,24},{24,16},{1,9},{9,1},{17,25},{25,17},{2,10},{10... | collective-permute-start | bytes 4325384 | tf_op jit(solution)/shard_map/ppermute | solution.py:835
  (213 other events, 3463.9 us)
Sparse Core Ops, SparseCore 0:
  90.2 52.4 all-gather.6
  144.8 132.1 all-gather.4
  563.6 61.3 reduce-scatter.3
  726.5 170.1 reduce-scatter.5
  1026.2 76.5 reduce-scatter.7
